TPU v7x, 256 devices: a whole 4x4x8 slice. The times are simulated.
256 devices in a mesh: gx: 4 (over x), gy: 64 (over z, y, core).
Axes of the slice: x: 4, y: 4, z: 8, core: 2. Of those that a mesh axis runs over, the one named last changes fastest.
Arguments:
- right_side: float32 [4096, 64, 128], P(('gx', 'gy')), may hold values from -6 to 6
- diagonal_matrices: float32 [4096, 64, 64], P(('gx', 'gy')), as said below
- nearby_coupling_blocks: float32 [4096, 4, 64, 64], P(('gx', 'gy'))
- neighbors: int32 [4096, 4], P(('gx', 'gy')), may hold values from 0 to 4095, as said below
- pairs: int32 [256, 3, 2, 8], P(('gx', 'gy')), may hold values from -1 to 15, as said below
- remote_coupling_blocks: float32 [256, 3, 8, 64, 64], P(('gx', 'gy'))
Outputs:
- solution: float32 [4096, 64, 128], P(('gx', 'gy'))
- residual: float32 [4096, 64, 128], P(('gx', 'gy'))
Inputs may be any that keep to these rules, and one draw needn't show every extreme that they name: Every neighbour of a block lies in the block's own range of 16 blocks, is not the block itself, and the pattern is symmetric slot by slot: if neighbors[i, k] = j then neighbors[j, k] = i. For device d and level e, with partner p = d xor 2^e: pairs[d, e, 0] lists distinct local blocks of d and pairs[d, e, 1] local blocks of p, with pairs[p, e, 0, t] = pairs[d, e, 1, t] and pairs[p, e, 1, t] = pairs[d, e, 0, t]; a pair of devices uses the same leading count c of slots, the rest are -1 in both rows; at every level some pair uses all 8 slots. The operator assembled from diagonal_matrices, nearby_coupling_blocks and remote_coupling_blocks is symmetric and positive definite.
All inputs are finite; a program needn't handle non-finite values.
Results may differ from a plain program's by a relative error of at most 0.0003.
Values sent between devices are 32-bit elements; how exact they have to be, the bound alone decides.
A program may use at most 64 MiB of HBM per device.

v0:
```python
import jax
import jax.numpy as jnp
from jax import lax
from jax.sharding import PartitionSpec as P

CROSS = 3
ITERS = 3


EXACT_ACCURACY = lax.Precision.HIGHEST


def partner(value, axis, apart):
    return lax.ppermute(value, axis, [(i, i ^ 1 << apart) for i in range(lax.axis_size(axis))])


def local(
    right_side, diagonal_matrices, nearby_coupling_blocks, neighbors, pairs, remote_coupling_blocks
):
    blocks_dev = right_side.shape[0]
    first_block = lax.axis_index(("gx", "gy")) * blocks_dev
    local_ids = neighbors - first_block
    positions = jnp.arange(blocks_dev, dtype=jnp.int32)
    self_onehot = [
        (pairs[0, octree_bit_depth, 0][:, None] == positions[None, :]).astype(jnp.float32)
        for octree_bit_depth in range(CROSS)
    ]
    remote_onehot = [
        (pairs[0, octree_bit_depth, 1][:, None] == positions[None, :]).astype(jnp.float32)
        for octree_bit_depth in range(CROSS)
    ]

    def operate(input_vector):
        operator_result = jnp.einsum(
            "ejg,egw->ejw", diagonal_matrices, input_vector, precision=EXACT_ACCURACY
        )
        gathered_values = input_vector[local_ids]
        operator_result = operator_result + jnp.einsum(
            "fdyw,fdwt->fyt", nearby_coupling_blocks, gathered_values, precision=EXACT_ACCURACY
        )
        for octree_bit_depth in range(CROSS):
            complete_voxel_field = partner(input_vector, ("gx", "gy"), octree_bit_depth)
            received_vector = jnp.einsum(
                "zo,ouj->zuj",
                remote_onehot[octree_bit_depth],
                complete_voxel_field,
                precision=EXACT_ACCURACY,
            )
            coupled_output = jnp.einsum(
                "vxz,vzp->vxp",
                remote_coupling_blocks[0, octree_bit_depth],
                received_vector,
                precision=EXACT_ACCURACY,
            )
            operator_result = operator_result + jnp.einsum(
                "fx,fzg->xzg",
                self_onehot[octree_bit_depth],
                coupled_output,
                precision=EXACT_ACCURACY,
            )
        return operator_result

    solution = jnp.zeros_like(right_side)
    residual = right_side
    res_image = operate(residual)
    direction = residual
    dir_image = res_image
    dir_image2 = res_image
    gamma_prev = None
    step_prev = None
    for iteration in range(ITERS):
        gamma_now, delta_now = lax.psum(
            (jnp.sum(residual * residual, axis=(0, 1)), jnp.sum(res_image * residual, axis=(0, 1))),
            ("gx", "gy"),
        )
        res_image2 = operate(res_image)
        if iteration == 0:
            step_len = gamma_now / delta_now
            direction = residual
            dir_image = res_image
            dir_image2 = res_image2
        else:
            ratio_now = gamma_now / gamma_prev
            step_len = gamma_now / (delta_now - ratio_now * gamma_now / step_prev)
            direction = residual + ratio_now[None, None, :] * direction
            dir_image = res_image + ratio_now[None, None, :] * dir_image
            dir_image2 = res_image2 + ratio_now[None, None, :] * dir_image2
        solution = solution + step_len[None, None, :] * direction
        residual = residual - step_len[None, None, :] * dir_image
        res_image = res_image - step_len[None, None, :] * dir_image2
        gamma_prev = gamma_now
        step_prev = step_len
    return (solution, residual)


def solution(mesh):
    in_specs = (
        P(("gx", "gy"), None, None),
        P(("gx", "gy"), None, None),
        P(("gx", "gy"), None, None, None),
        P(("gx", "gy"), None),
        P(("gx", "gy"), None, None, None),
        P(("gx", "gy"), None, None, None, None),
    )
    out_specs = (P(("gx", "gy"), None, None), P(("gx", "gy"), None, None))
    return jax.shard_map(local, mesh=mesh, in_specs=in_specs, out_specs=out_specs, check_vma=False)
```

profile of v0, /device:TPU:1, one launch (start us, length us, event | category | flops | bytes accessed | tf_op | source)
XLA Modules:
  0.0 322.4 jit_solution(11685125224333735654)
XLA Ops:
  0.6 2.2 collective-permute-start.1
  2.9 1.2 collective-permute-start
  4.1 2.4 collective-permute-start.2
  6.4 0.7 compare_select_fusion
  7.3 3.1 gather_fusion
  10.4 3.9 %convolution_bitcast_fusion.2 = f32[16,64,128]{2,1,0:T(8,128)S(1)} fusion(f32[16,4,64,128]{3,2,1,0:T(8,128)} %bitcast.139, f32[16,4,64,64]{3,2,1,0:T(8,128)S(1)} %copy-done), kind=kOutput, calls=%fused_computation.5 | convolution fusion | flops 402653184 | bytes 3670016 | tf_op jit(solution)/shard_map/fdyw,fdwt->fyt/dot_general | solution.py:38
  14.3 1.6 fusion.28
  16.4 0.6 fusion.30
  17.0 0.4 fusion.66
  17.4 10.8 %collective-permute-done.2 = f32[16,64,128]{2,1,0:T(8,128)S(1)} collective-permute-done((f32[16,64,128]{2,1,0:T(8,128)}, f32[16,64,128]{2,1,0:T(8,128)S(1)}, u32[]{:S(2)}, u32[]{:S(2)}) %collective-permute-start.2) | collective-permute-done | bytes 524320 | tf_op jit(solution)/shard_map/ppermute | solution.py:14
  28.3 0.6 fusion.26
  28.9 0.4 fusion.50
  29.3 0.5 fusion.52
  29.8 0.5 fusion.60
  30.3 0.5 fusion.44
  30.9 1.1 multiply_reduce_fusion.4
  32.1 1.7 collective-permute-start.3
  33.8 1.1 collective-permute-start.5
  34.9 2.0 gather_fusion.1
  36.9 4.5 %convolution_bitcast_fusion.1 = f32[16,128,64]{1,2,0:T(8,128)} fusion(f32[16,4,64,128]{3,2,1,0:T(8,128)} %bitcast.140, f32[16,4,64,64]{3,2,1,0:T(8,128)S(1)} %copy-done), kind=kOutput, calls=%fused_computation.4 | convolution fusion | flops 402653184 | bytes 3670016 | tf_op jit(solution)/shard_map/fdyw,fdwt->fyt/dot_general | solution.py:38
  41.4 86.6 %all-reduce.2 = (f32[128]{0:T(128)S(1)}, f32[128]{0:T(128)S(1)}) all-reduce(f32[128]{0:T(128)S(1)} %get-tuple-element.7, f32[128]{0:T(128)S(1)} %get-tuple-element.6), channel_id=1, replica_groups=mesh['gx'=4,'gy'=64] {'gx','gy'}, use_global_device_ids=true, to_apply=%region_1.0 | all-reduce | flops 256 | bytes 2048 | tf_op jit(solution)/shard_map/psum | solution.py:72
  128.1 1.7 fusion.22
  129.8 1.3 fusion.56
  131.1 1.6 fusion.24
  132.8 0.4 fusion.64
  133.2 0.5 fusion.40
  133.7 0.5 fusion.42
  134.3 1.6 fusion.20
  135.9 0.4 fusion.48
  136.3 0.5 fusion.38
  136.9 2.4 multiply_reduce_fusion.2
  139.2 0.8 collective-permute-start.7
  140.0 3.1 gather_fusion.2
  143.1 1.0 collective-permute-start.6
  144.1 2.5 collective-permute-start.8
  146.6 84.5 %all-reduce.1 = (f32[128]{0:T(128)S(1)}, f32[128]{0:T(128)S(1)}) all-reduce(f32[128]{0:T(128)S(1)} %get-tuple-element.5, f32[128]{0:T(128)S(1)} %get-tuple-element.4), channel_id=1, replica_groups=mesh['gx'=4,'gy'=64] {'gx','gy'}, use_global_device_ids=true, to_apply=%region_5.0 | all-reduce | flops 256 | bytes 2048 | tf_op jit(solution)/shard_map/psum | solution.py:72
  231.1 3.9 %convolution_bitcast_fusion = f32[16,128,64]{1,2,0:T(8,128)S(1)} fusion(f32[16,4,64,128]{3,2,1,0:T(8,128)} %bitcast.138, f32[16,4,64,64]{3,2,1,0:T(8,128)S(1)} %copy-done), kind=kOutput, calls=%fused_computation.3 | convolution fusion | flops 402653184 | bytes 3670016 | tf_op jit(solution)/shard_map/fdyw,fdwt->fyt/dot_general | solution.py:38
  235.0 1.6 fusion.16
  237.1 1.6 fusion.18
  238.7 0.4 fusion.62
  239.1 0.5 fusion.34
  239.7 0.5 fusion.36
  240.2 1.6 fusion.14
  241.8 0.4 fusion.46
  242.3 0.5 fusion.32
  242.8 3.5 %multiply_reduce_fusion = (f32[128]{0:T(128)S(1)}, f32[128]{0:T(128)S(1)}, f32[16,64,128]{2,1,0:T(8,128)}, f32[16,64,128]{2,1,0:T(8,128)}) fusion(f32[16,64,128]{2,1,0:T(8,128)S(1)} %copy-done.8, f32[16,64,128]{2,1,0:T(8,128)} %get-tuple-element.20, f32[16,64,128]{2,1,0:T(8,128)S(1)} %get-tuple-element.30, f32[128]{0:T(128)S(1)} %get-tuple-element.19, ...), kind=kOutput, calls=%fused_computation.43 | convolution fusion | flops 102760192 | bytes 5507072 | tf_op jit(solution)/shard_map/ejg,egw->ejw/dot_general | solution.py:34
  246.3 73.2 %all-reduce = (f32[128]{0:T(128)S(1)}, f32[128]{0:T(128)S(1)}) all-reduce(f32[128]{0:T(128)S(1)} %get-tuple-element.3, f32[128]{0:T(128)S(1)} %get-tuple-element.2), channel_id=1, replica_groups=mesh['gx'=4,'gy'=64] {'gx','gy'}, use_global_device_ids=true, to_apply=%region_9.0 | all-reduce | flops 256 | bytes 2048 | tf_op jit(solution)/shard_map/psum | solution.py:72
  319.5 2.8 multiply_subtract_fusion
  (42 shorter events, 1.2 us)
Async XLA Ops:
  0.6 9.7 %copy-start = (f32[16,4,64,64]{3,2,1,0:T(8,128)S(1)}, f32[16,4,64,64]{3,2,1,0:T(8,128)}, u32[]{:S(2)}) copy-start(f32[16,4,64,64]{3,2,1,0:T(8,128)} %param.8) | copy-start | bytes 3145732
  0.6 13.7 %collective-permute-start.1 = (f32[16,64,128]{2,1,0:T(8,128)}, f32[16,64,128]{2,1,0:T(8,128)}, u32[]{:S(2)}, u32[]{:S(2)}) collective-permute-start(f32[16,64,128]{2,1,0:T(8,128)} %param.6), channel_id=1, source_target_pairs={{0,2},{1,3},{2,0},{3,1},{4,6},{5,7},{6,4},{7,5},{8,10},{9,11},{10,... | collective-permute-start | bytes 1572872 | tf_op jit(solution)/shard_map/ppermute | solution.py:14
  2.9 13.5 %collective-permute-start = (f32[16,64,128]{2,1,0:T(8,128)}, f32[16,64,128]{2,1,0:T(8,128)S(1)}, u32[]{:S(2)}, u32[]{:S(2)}) collective-permute-start(f32[16,64,128]{2,1,0:T(8,128)} %param.6), channel_id=1, source_target_pairs={{0,1},{1,0},{2,3},{3,2},{4,5},{5,4},{6,7},{7,6},{8,9},{9,8},{10,11... | collective-permute-start | bytes 1572872 | tf_op jit(solution)/shard_map/ppermute | solution.py:14
  4.1 24.2 %collective-permute-start.2 = (f32[16,64,128]{2,1,0:T(8,128)}, f32[16,64,128]{2,1,0:T(8,128)S(1)}, u32[]{:S(2)}, u32[]{:S(2)}) collective-permute-start(f32[16,64,128]{2,1,0:T(8,128)} %param.6), channel_id=1, source_target_pairs={{0,4},{1,5},{2,6},{3,7},{4,0},{5,1},{6,2},{7,3},{8,12},{9,13},{10,... | collective-permute-start | bytes 1572872 | tf_op jit(solution)/shard_map/ppermute | solution.py:14
  10.4 3.9 %copy-start.11 = (s32[1,3,2,8]{3,2,1,0:T(2,128)S(1)}, s32[1,3,2,8]{3,2,1,0:T(2,128)}, u32[]{:S(2)}) copy-start(s32[1,3,2,8]{3,2,1,0:T(2,128)} %param.10) | copy-start | bytes 580
  10.4 5.6 %copy-start.2 = (f32[1,3,8,64,64]{4,3,2,1,0:T(8,128)S(1)}, f32[1,3,8,64,64]{4,3,2,1,0:T(8,128)}, u32[]{:S(2)}) copy-start(f32[1,3,8,64,64]{4,3,2,1,0:T(8,128)} %param.11) | copy-start | bytes 1179652
  17.4 13.5 %copy-start.1 = (f32[16,64,128]{2,1,0:T(8,128)S(1)}, f32[16,64,128]{2,1,0:T(8,128)}, u32[]{:S(2)}) copy-start(f32[16,64,128]{2,1,0:T(8,128)} %param.6) | copy-start | bytes 1572868
  17.4 13.5 %copy-start.5 = (f32[16,64,64]{2,1,0:T(8,128)S(1)}, f32[16,64,64]{2,1,0:T(8,128)}, u32[]{:S(2)}) copy-start(f32[16,64,64]{2,1,0:T(8,128)} %param.7) | copy-start | bytes 786436
  32.0 96.0 %collective-permute-start.4 = (f32[16,64,128]{2,1,0:T(8,128)S(1)}, f32[16,64,128]{2,1,0:T(8,128)}, u32[]{:S(2)}, u32[]{:S(2)}) collective-permute-start(f32[16,64,128]{2,1,0:T(8,128)S(1)} %get-tuple-element.30), channel_id=1, source_target_pairs={{0,2},{1,3},{2,0},{3,1},{4,6},{5,7},{6,4},{7,5},{8,10},{9,11},{10,... | collective-permute-start | bytes 1572872 | tf_op jit(solution)/shard_map/ppermute | solution.py:14
  32.1 99.0 %collective-permute-start.3 = (f32[16,64,128]{2,1,0:T(8,128)S(1)}, f32[16,64,128]{2,1,0:T(8,128)}, u32[]{:S(2)}, u32[]{:S(2)}) collective-permute-start(f32[16,64,128]{2,1,0:T(8,128)S(1)} %get-tuple-element.30), channel_id=1, source_target_pairs={{0,1},{1,0},{2,3},{3,2},{4,5},{5,4},{6,7},{7,6},{8,9},{9,8},{10,11... | collective-permute-start | bytes 1572872 | tf_op jit(solution)/shard_map/ppermute | solution.py:14
  33.8 100.5 %collective-permute-start.5 = (f32[16,64,128]{2,1,0:T(8,128)S(1)}, f32[16,64,128]{2,1,0:T(8,128)}, u32[]{:S(2)}, u32[]{:S(2)}) collective-permute-start(f32[16,64,128]{2,1,0:T(8,128)S(1)} %get-tuple-element.30), channel_id=1, source_target_pairs={{0,4},{1,5},{2,6},{3,7},{4,0},{5,1},{6,2},{7,3},{8,12},{9,13},{10,... | collective-permute-start | bytes 1572872 | tf_op jit(solution)/shard_map/ppermute | solution.py:14
  128.0 4.7 %copy-start.3 = (f32[1,3,8,64,64]{4,3,2,1,0:T(8,128)S(1)}, f32[1,3,8,64,64]{4,3,2,1,0:T(8,128)}, u32[]{:S(2)}) copy-start(f32[1,3,8,64,64]{4,3,2,1,0:T(8,128)} %param.11) | copy-start | bytes 1179652
  133.2 3.7 %copy-start.6 = (f32[16,64,64]{2,1,0:T(8,128)S(1)}, f32[16,64,64]{2,1,0:T(8,128)}, u32[]{:S(2)}) copy-start(f32[16,64,64]{2,1,0:T(8,128)} %param.7) | copy-start | bytes 786436
  133.2 3.7 %copy-start.9 = (f32[16,128,64]{1,2,0:T(8,128)S(1)}, f32[16,128,64]{1,2,0:T(8,128)}, u32[]{:S(2)}) copy-start(f32[16,128,64]{1,2,0:T(8,128)} %convolution_bitcast_fusion.1) | copy-start | bytes 1572868
  139.2 95.8 %collective-permute-start.7 = (f32[16,64,128]{2,1,0:T(8,128)}, f32[16,64,128]{2,1,0:T(8,128)}, u32[]{:S(2)}, u32[]{:S(2)}) collective-permute-start(f32[16,64,128]{2,1,0:T(8,128)} %get-tuple-element.20), channel_id=1, source_target_pairs={{0,2},{1,3},{2,0},{3,1},{4,6},{5,7},{6,4},{7,5},{8,10},{9,11},{10,... | collective-permute-start | bytes 1572872 | tf_op jit(solution)/shard_map/ppermute | solution.py:14
  143.1 93.9 %collective-permute-start.6 = (f32[16,64,128]{2,1,0:T(8,128)}, f32[16,64,128]{2,1,0:T(8,128)}, u32[]{:S(2)}, u32[]{:S(2)}) collective-permute-start(f32[16,64,128]{2,1,0:T(8,128)} %get-tuple-element.20), channel_id=1, source_target_pairs={{0,1},{1,0},{2,3},{3,2},{4,5},{5,4},{6,7},{7,6},{8,9},{9,8},{10,11... | collective-permute-start | bytes 1572872 | tf_op jit(solution)/shard_map/ppermute | solution.py:14
  144.1 96.1 %collective-permute-start.8 = (f32[16,64,128]{2,1,0:T(8,128)}, f32[16,64,128]{2,1,0:T(8,128)}, u32[]{:S(2)}, u32[]{:S(2)}) collective-permute-start(f32[16,64,128]{2,1,0:T(8,128)} %get-tuple-element.20), channel_id=1, source_target_pairs={{0,4},{1,5},{2,6},{3,7},{4,0},{5,1},{6,2},{7,3},{8,12},{9,13},{10,... | collective-permute-start | bytes 1572872 | tf_op jit(solution)/shard_map/ppermute | solution.py:14
  231.1 5.6 %copy-start.4 = (f32[1,3,8,64,64]{4,3,2,1,0:T(8,128)S(1)}, f32[1,3,8,64,64]{4,3,2,1,0:T(8,128)}, u32[]{:S(2)}) copy-start(f32[1,3,8,64,64]{4,3,2,1,0:T(8,128)} %param.11) | copy-start | bytes 1179652
  239.1 3.7 %copy-start.7 = (f32[16,64,64]{2,1,0:T(8,128)S(1)}, f32[16,64,64]{2,1,0:T(8,128)}, u32[]{:S(2)}) copy-start(f32[16,64,64]{2,1,0:T(8,128)} %param.7) | copy-start | bytes 786436
  239.1 3.7 %copy-start.8 = (f32[16,64,128]{2,1,0:T(8,128)S(1)}, f32[16,64,128]{2,1,0:T(8,128)}, u32[]{:S(2)}) copy-start(f32[16,64,128]{2,1,0:T(8,128)} %get-tuple-element.21) | copy-start | bytes 1572868
  239.1 3.7 %copy-start.10 = (f32[16,64,128]{2,1,0:T(8,128)S(1)}, f32[16,64,128]{2,1,0:T(8,128)}, u32[]{:S(2)}) copy-start(f32[16,64,128]{2,1,0:T(8,128)} %get-tuple-element.31) | copy-start | bytes 1572868
where the time goes:
time: 323 us; the launch traced here: 322 us
  blocking collectives  244 us (76%)
  matrix products  41.3 us (13%)
  starting transfers between devices  12.9 us (4%)
  waiting for transfers between devices  10.9 us (3%)
  local copies, waits for them, and re-layouts  8.38 us (3%)
  other arithmetic  3.55 us (1%)
    psum x3, blocking collectives, local(): lax.psum((jnp.sum(residual * residual, axis=(0, 1)), jnp.sum(res_image *...  244 us
    ppermute x9, starting transfers between devices, partner(): lax.ppermute(value, axis, [(i, i ^ 1 << apart) for i in range(lax.axis_si...  12.9 us
    dot_general x9, matrix products, operate(): jnp.einsum('zo,ouj->zuj', remote_onehot[octree_bit_depth], complete_voxel...  12.6 us
    dot_general x3, matrix products, operate(): jnp.einsum('fdyw,fdwt->fyt', nearby_coupling_blocks, gathered_values, pre...  12.3 us
    ppermute x9, waiting for transfers between devices, partner(): lax.ppermute(value, axis, [(i, i ^ 1 << apart) for i in range(lax.axis_si...  10.9 us
    gather x3, local copies, waits for them, and re-layouts, operate(): gathered_values = input_vector[local_ids]  8.14 us
    dot_general x3, matrix products, operate(): jnp.einsum('ejg,egw->ejw', diagonal_matrices, input_vector, precision=EXA...  7 us
  transfers between devices with their start and end apart: 9, of which 1 were waited for; matrix products, arithmetic and copies ran while one was open for 11% of the time, Pallas kernels for 0%

commit v1 on v0

v1 whole, which is shorter than its diff:
```python
import functools

import jax
import jax.numpy as jnp
from jax import lax
from jax.experimental import pallas as pl
from jax.experimental.pallas import tpu as pltpu
from jax.sharding import PartitionSpec as P

CROSS = 3
SLOTS = 8
HALF = SLOTS // 2
LOCAL = 4
BLOCKS = 16
WIDTH = 64
RHS = 128
SOURCES = LOCAL + 1
DEPTH = 3 * WIDTH
MESH = pl.DeviceIdType.MESH
LEVEL_ORDER = (2, 1, 0)


def tree_sum(parts):
    while len(parts) > 1:
        parts = [parts[i] + parts[i + 1] for i in range(0, len(parts), 2)]
    return parts[0]


def split(value):
    high = value.astype(jnp.bfloat16)
    low = (value - high.astype(jnp.float32)).astype(jnp.bfloat16)
    return high, low


def fold(value):
    return jnp.sum(value.reshape(WIDTH // 8, 8, RHS), axis=0)


def kernel(
    nx, nz,
    neighbors, pairs, right_side, diagonal, nearby, remote,
    solution, residual,
    w0, w1, z0, z1, r1, x_high, x_low, near_lhs, far_lhs, coupled,
    sent, received, first_sums, second_sums, inverse,
    send_sem, recv_sem, first_send, first_recv, second_send, second_recv,
):
    gx = lax.axis_index("gx")
    gy = lax.axis_index("gy")
    z, y, core = gy // 8, (gy // 2) % 4, gy % 2
    n1, n2 = 2 * nz, 4 * nx
    me1, me2 = z * 2 + core, gx * 4 + y

    def first_peer(k):
        other = jnp.bitwise_xor(me1, k)
        return gx, ((other // 2) * 4 + y) * 2 + other % 2

    def second_peer(k):
        other = jnp.bitwise_xor(me2, k)
        return other // 4, (z * 4 + other % 4) * 2 + core

    barrier = pltpu.get_barrier_semaphore()

    def greet(peer):
        def one(k, carry):
            pl.semaphore_signal(barrier, inc=1, device_id=peer(k), device_id_type=MESH)
            return carry
        return one

    lax.fori_loop(1, n1, greet(first_peer), 0)
    lax.fori_loop(1, n2, greet(second_peer), 0)
    pl.semaphore_wait(barrier, n1 + n2 - 2)

    bits = [(gy // (1 << e)) % 2 for e in range(CROSS)]

    def slot_copy(op, e, t):
        return pltpu.make_async_remote_copy(
            src_ref=sent.at[op, e, t],
            dst_ref=received.at[op, e, t],
            send_sem=send_sem.at[op, e, t],
            recv_sem=recv_sem.at[op, e, t],
            device_id=(gx, jnp.bitwise_xor(gy, 1 << e)),
            device_id_type=MESH,
        )

    def send_all(op, source):
        for half in range(2):
            def one(q, carry):
                for e in LEVEL_ORDER:
                    base = HALF * (1 - bits[e]) if half == 0 else HALF * bits[e]
                    t = base + q
                    own = jnp.maximum(pairs[0, e, 0, t], 0)
                    sent[op, e, t] = source[own]
                    slot_copy(op, e, t).start()
                return carry
            lax.fori_loop(0, HALF, one, 0)

    def sum_copy(index, stage, k):
        buffer, sends, recvs, peer = (
            (first_sums, first_send, first_recv, first_peer),
            (second_sums, second_send, second_recv, second_peer),
        )[stage]
        return pltpu.make_async_remote_copy(
            src_ref=buffer.at[index, 0],
            dst_ref=buffer.at[index, k],
            send_sem=sends.at[index],
            recv_sem=recvs.at[index],
            device_id=peer(k),
            device_id_type=MESH,
        )

    def sum_all_wait(index, stage):
        buffer, sends, recvs, peer = (
            (first_sums, first_send, first_recv, first_peer),
            (second_sums, second_send, second_recv, second_peer),
        )[stage]
        n = (n1, n2)[stage]
        return pltpu.make_async_remote_copy(
            src_ref=buffer.at[index, pl.ds(1, n - 1)],
            dst_ref=buffer.at[index, pl.ds(1, n - 1)],
            send_sem=sends.at[index],
            recv_sem=recvs.at[index],
            device_id=peer(1),
            device_id_type=MESH,
        )

    def sum_start(index, stage, value):
        buffer, n = ((first_sums, n1), (second_sums, n2))[stage]
        buffer[index, 0] = value

        def one(k, carry):
            sum_copy(index, stage, k).start()
            return carry
        lax.fori_loop(1, n, one, 0)

    def sum_finish(index, stage):
        buffer, n = ((first_sums, n1), (second_sums, n2))[stage]
        sum_all_wait(index, stage).wait_recv()
        return tree_sum([buffer[index, k] for k in range(n)])

    def rows_of(values):
        rows = [jnp.sum(v, axis=0, keepdims=True) for v in values]
        rows += [jnp.zeros((8 - len(rows), RHS), jnp.float32)] if len(rows) < 8 else []
        return jnp.concatenate(rows, axis=0)

    def split_all(source):
        def one(i, carry):
            high, low = split(source[i])
            x_high[i] = high
            x_low[i] = low
            return carry
        lax.fori_loop(0, BLOCKS, one, 0)

    def near_product(i):
        sources = [i] + [jnp.bitwise_and(neighbors[i, k], BLOCKS - 1) for k in range(LOCAL)]
        highs = [x_high[j] for j in sources]
        lows = [x_low[j] for j in sources]
        rhs = jnp.concatenate([h for high in highs for h in (high, high)] + lows, axis=0)
        return jnp.dot(near_lhs[i][:, : SOURCES * DEPTH], rhs, preferred_element_type=jnp.float32)

    def far_product(op, e, t):
        slot_copy(op, e, t).wait_recv()
        high, low = split(received[op, e, t])
        rhs = jnp.concatenate([high, high, low], axis=0)
        product = jnp.dot(far_lhs[e, t][:, :DEPTH], rhs, preferred_element_type=jnp.float32)
        coupled[e, t] = product
        return product

    def far_half(op, half):
        def one(q, carry):
            for e in reversed(LEVEL_ORDER):
                far_product(op, e, q + (HALF * bits[e] if half == 0 else HALF * (1 - bits[e])))
            return carry
        lax.fori_loop(0, HALF, one, 0)

    def far_rows(i):
        return [coupled[e, inverse[e * BLOCKS + i]] for e in range(CROSS)]

    zero = jnp.zeros((8, RHS), jnp.float32)

    send_all(0, right_side)

    lane = lax.broadcasted_iota(jnp.int32, (WIDTH, 2 * WIDTH), 1)

    def both(block):
        twice = jnp.concatenate([block, block], axis=1)
        high = twice.astype(jnp.bfloat16).astype(jnp.float32)
        return jnp.where(lane < WIDTH, high, twice - high).astype(jnp.bfloat16)

    def near_setup(i, carry):
        blocks = [diagonal[i]] + [nearby[i, k] for k in range(LOCAL)]
        for s, block in enumerate(blocks):
            near_lhs[i, :, pl.ds(s * 2 * WIDTH, 2 * WIDTH)] = both(block)
        for s in range(0, SOURCES, 2):
            pair = jnp.concatenate([blocks[s], blocks[min(s + 1, SOURCES - 1)]], axis=1)
            near_lhs[i, :, pl.ds((SOURCES * 2 + s) * WIDTH, 2 * WIDTH)] = pair.astype(jnp.bfloat16)
        return carry

    lax.fori_loop(0, BLOCKS, near_setup, 0)

    def far_setup(t, carry):
        for e in range(CROSS):
            block = remote[0, e, t]
            far_lhs[e, t, :, pl.ds(0, 2 * WIDTH)] = both(block)
            twice = jnp.concatenate([block, block], axis=1)
            far_lhs[e, t, :, pl.ds(2 * WIDTH, 2 * WIDTH)] = twice.astype(jnp.bfloat16)
        return carry

    lax.fori_loop(0, SLOTS, far_setup, 0)

    for e in range(CROSS):
        coupled[e, SLOTS] = jnp.zeros((WIDTH, RHS), jnp.float32)
        owns = [pairs[0, e, 0, t] for t in range(SLOTS)]

        def invert(i, carry):
            found = jnp.int32(SLOTS)
            for t in range(SLOTS):
                found = jnp.where(owns[t] == i, jnp.int32(t), found)
            inverse[e * BLOCKS + i] = found
            return carry
        lax.fori_loop(0, BLOCKS, invert, 0)

    split_all(right_side)

    def w0_near(i, carry):
        w0[i] = near_product(i)
        return carry

    lax.fori_loop(0, BLOCKS, w0_near, 0)
    far_half(0, 0)
    far_half(0, 1)

    def w0_join(i, carry):
        gamma, delta = carry
        r = right_side[i]
        w = w0[i] + tree_sum(far_rows(i) + [jnp.zeros_like(r)])
        w0[i] = w
        return gamma + fold(r * r), delta + fold(w * r)

    gamma, delta = lax.fori_loop(0, BLOCKS, w0_join, (zero, zero))

    send_all(1, w0)
    sum_start(0, 0, rows_of([gamma, delta]))
    split_all(w0)

    def z0_near(i, carry):
        z0[i] = near_product(i)
        return carry

    lax.fori_loop(0, BLOCKS, z0_near, 0)
    sum_start(0, 1, sum_finish(0, 0))
    far_half(1, 0)
    far_half(1, 1)
    totals = sum_finish(0, 1)
    gamma0, delta0 = totals[0:1], totals[1:2]
    step0 = gamma0 / delta0

    def z0_join(i, carry):
        zz = z0[i] + tree_sum(far_rows(i) + [jnp.zeros((WIDTH, RHS), jnp.float32)])
        z0[i] = zz
        w1[i] = w0[i] - step0 * zz
        return carry

    lax.fori_loop(0, BLOCKS, z0_join, 0)

    send_all(2, w1)

    def gram(i, carry):
        wa, wb, zz = w0[i], w1[i], z0[i]
        r = right_side[i] - step0 * wa
        r1[i] = r
        terms = (r * r, r * wb, r * wa, wb * wb, wb * wa, wa * wa, wb * zz, wa * zz)
        return tuple(c + fold(t) for c, t in zip(carry, terms))

    sums = lax.fori_loop(0, BLOCKS, gram, (zero,) * 8)
    sum_start(1, 0, rows_of(sums))
    split_all(w1)

    def z1_near(i, energy):
        product = near_product(i)
        z1[i] = product
        return energy + fold(product * w1[i])

    energy = lax.fori_loop(0, BLOCKS, z1_near, zero)

    def energy_half(q, carry):
        for e in reversed(LEVEL_ORDER):
            t = q + HALF * bits[e]
            product = far_product(2, e, t)
            twice = jnp.where(pairs[0, e, 0, t] >= 0, 2.0 * fold(product * sent[2, e, t]), 0.0)
            carry = carry + twice
        return carry

    energy = lax.fori_loop(0, HALF, energy_half, energy)
    sum_start(2, 0, rows_of([energy]))
    sum_start(1, 1, sum_finish(1, 0))
    far_half(2, 1)
    sum_start(2, 1, sum_finish(2, 0))
    totals = sum_finish(1, 1)
    gamma1, delta1, rw0, w1w1, w1w0, w0w0, w1z0, w0z0 = [totals[k : k + 1] for k in range(8)]
    ratio1 = gamma1 / gamma0
    step1 = gamma1 / (delta1 - ratio1 * gamma1 / step0)

    def z1_join(i, carry):
        zz = z1[i] + tree_sum(far_rows(i) + [jnp.zeros((WIDTH, RHS), jnp.float32)])
        r, wa, wb, r0 = r1[i], w0[i], w1[i], right_side[i]
        p1 = r + ratio1 * r0
        ap1 = wb + ratio1 * wa
        solution[i] = step0 * r0 + step1 * p1
        residual[i] = r - step1 * ap1
        z1[i] = wb - step1 * (zz + ratio1 * z0[i])
        r1[i] = p1
        w1[i] = ap1
        return carry

    lax.fori_loop(0, BLOCKS, z1_join, 0)

    w1aw1 = sum_finish(2, 1)[0:1]
    gamma2 = (
        gamma1
        - 2.0 * step1 * (delta1 + ratio1 * rw0)
        + step1 * step1 * (w1w1 + 2.0 * ratio1 * w1w0 + ratio1 * ratio1 * w0w0)
    )
    delta2 = (
        delta1
        - 2.0 * step1 * (w1w1 + ratio1 * w1w0)
        + step1 * step1 * (w1aw1 + 2.0 * ratio1 * w1z0 + ratio1 * ratio1 * w0z0)
    )
    ratio2 = gamma2 / gamma1
    step2 = gamma2 / (delta2 - ratio2 * gamma2 / step1)

    def last(i, carry):
        r2 = residual[i]
        solution[i] = solution[i] + step2 * (r2 + ratio2 * r1[i])
        residual[i] = r2 - step2 * (z1[i] + ratio2 * w1[i])
        return carry

    lax.fori_loop(0, BLOCKS, last, 0)

    for op in range(3):
        def drain(t, carry):
            for e in range(CROSS):
                slot_copy(op, e, t).wait_send()
            return carry
        lax.fori_loop(0, SLOTS, drain, 0)
        for stage in range(2):
            sum_all_wait(op, stage).wait_send()


def solution(mesh):
    nx, nz = mesh.shape["gx"], mesh.shape["gy"] // 8
    n1, n2 = 2 * nz, 4 * nx

    def local(right_side, diagonal_matrices, nearby_coupling_blocks, neighbors, pairs, remote_coupling_blocks):
        field = (BLOCKS, WIDTH, RHS)
        vmem = pl.BlockSpec(memory_space=pltpu.VMEM)
        smem = pl.BlockSpec(memory_space=pltpu.SMEM)
        f32, bf16 = jnp.float32, jnp.bfloat16
        return pl.pallas_call(
            functools.partial(kernel, nx, nz),
            out_shape=(jax.ShapeDtypeStruct(field, f32), jax.ShapeDtypeStruct(field, f32)),
            in_specs=[smem, smem, vmem, vmem, vmem, vmem],
            out_specs=(vmem, vmem),
            scratch_shapes=[pltpu.VMEM(field, f32)] * 5
            + [
                pltpu.VMEM(field, bf16),
                pltpu.VMEM(field, bf16),
                pltpu.VMEM((BLOCKS, WIDTH, 1024), bf16),
                pltpu.VMEM((CROSS, SLOTS, WIDTH, 256), bf16),
                pltpu.VMEM((CROSS, SLOTS + 1, WIDTH, RHS), f32),
                pltpu.VMEM((3, CROSS, SLOTS, WIDTH, RHS), f32),
                pltpu.VMEM((3, CROSS, SLOTS, WIDTH, RHS), f32),
                pltpu.VMEM((3, n1, 8, RHS), f32),
                pltpu.VMEM((3, n2, 8, RHS), f32),
                pltpu.SMEM((CROSS * BLOCKS,), jnp.int32),
                pltpu.SemaphoreType.DMA((3, CROSS, SLOTS)),
                pltpu.SemaphoreType.DMA((3, CROSS, SLOTS)),
                pltpu.SemaphoreType.DMA((3,)),
                pltpu.SemaphoreType.DMA((3,)),
                pltpu.SemaphoreType.DMA((3,)),
                pltpu.SemaphoreType.DMA((3,)),
            ],
            compiler_params=pltpu.CompilerParams(
                collective_id=0, has_side_effects=True, vmem_limit_bytes=40 * 1024 * 1024
            ),
            name="relay",
        )(neighbors, pairs, right_side, diagonal_matrices, nearby_coupling_blocks, remote_coupling_blocks)

    wide = P(("gx", "gy"), None, None)
    return jax.shard_map(
        local,
        mesh=mesh,
        in_specs=(
            wide,
            wide,
            P(("gx", "gy"), None, None, None),
            P(("gx", "gy"), None),
            P(("gx", "gy"), None, None, None),
            P(("gx", "gy"), None, None, None, None),
        ),
        out_specs=(wide, wide),
        check_vma=False,
    )
```

time: 323 us -> 67.4 us (0.21)
  blocking collectives: 244 us -> 0 us
  Pallas kernels: 0 us -> 58.6 us
  matrix products: 41.3 us -> 0 us
  starting transfers between devices: 12.9 us -> 0 us
  waiting for transfers between devices: 10.9 us -> 0 us
  other arithmetic: 3.55 us -> 0 us
    psum x3 -> x0, blocking collectives: 244 us -> none  [local(): lax.psum((jnp.sum(residual * residual, axis=(0, 1)), jnp.sum(res_image *...]
    pallas_call x0 -> x1, Pallas kernels: none -> 58.6 us  [local(): pl.pallas_call(functools.partial(kernel, nx, nz), out_shape=(jax.ShapeDty...]
    dot_general x33 -> x0, matrix products: 41.3 us -> none  [the longest x9 12.6 us: operate(): jnp.einsum('zo,ouj->zuj', remote_onehot[octree_bit_depth], complete_voxel...]
    ppermute x9 -> x0, starting transfers between devices: 12.9 us -> none  [partner(): lax.ppermute(value, axis, [(i, i ^ 1 << apart) for i in range(lax.axis_si...]
    ppermute x9 -> x0, waiting for transfers between devices: 10.9 us -> none  [partner(): lax.ppermute(value, axis, [(i, i ^ 1 << apart) for i in range(lax.axis_si...]
    gather x3 -> x0, local copies, waits for them, and re-layouts: 8.14 us -> none  [operate(): gathered_values = input_vector[local_ids]]
    unnamed x24 -> x13, local copies, waits for them, and re-layouts: 0.07 us -> 7.84 us
  transfers between devices with their start and end apart: 9 -> 0, of which waited for: 1 -> 0; matrix products, arithmetic and copies ran while one was open for 11% -> 0% of each run, Pallas kernels for 0% -> 0%
where the time goes in v1:
time: 67.4 us; the launch traced here: 67.1 us
  Pallas kernels  58.6 us (87%)
  local copies, waits for them, and re-layouts  7.84 us (12%)
    pallas_call x1, Pallas kernels, local(): pl.pallas_call(functools.partial(kernel, nx, nz), out_shape=(jax.ShapeDty...  58.6 us
    unnamed x13, local copies, waits for them, and re-layouts  7.84 us

profile of v1, /device:TPU:1, one launch (start us, length us, event | category | flops | bytes accessed | tf_op | source)
XLA Modules:
  0.0 67.1 jit_solution(10291885844926437335)
XLA Ops:
  0.6 0.8 %copy.8.neighbors = s32[16,4]{1,0:T(8,128)S(1)} copy(s32[16,4]{0,1:T(4,128)} %param.9) | data formatting | bytes 512 | tf_op args[3]
  1.4 0.0 copy-start
  1.4 1.6 %copy-done = f32[16,4,64,64]{3,2,1,0:T(8,128)S(1)} copy-done((f32[16,4,64,64]{3,2,1,0:T(8,128)S(1)}, f32[16,4,64,64]{3,2,1,0:T(8,128)}, u32[]{:S(2)}) %copy-start) | copy-done | bytes 1048600
  3.0 0.0 copy-start.1
  3.0 1.1 %copy-done.1 = f32[1,3,8,64,64]{4,3,2,1,0:T(8,128)S(1)} copy-done((f32[1,3,8,64,64]{4,3,2,1,0:T(8,128)S(1)}, f32[1,3,8,64,64]{4,3,2,1,0:T(8,128)}, u32[]{:S(2)}) %copy-start.1) | copy-done | bytes 393240
  4.1 0.0 copy-start.2
  4.1 1.0 %copy-done.2 = f32[16,64,128]{2,1,0:T(8,128)S(1)} copy-done((f32[16,64,128]{2,1,0:T(8,128)S(1)}, f32[16,64,128]{2,1,0:T(8,128)}, u32[]{:S(2)}) %copy-start.2) | copy-done | bytes 524312
  5.2 0.0 copy-start.3
  5.2 1.0 %copy-done.3 = f32[16,64,64]{2,1,0:T(8,128)S(1)} copy-done((f32[16,64,64]{2,1,0:T(8,128)S(1)}, f32[16,64,64]{2,1,0:T(8,128)}, u32[]{:S(2)}) %copy-start.3) | copy-done | bytes 262168
  6.2 0.0 copy-start.4
  6.2 0.7 %copy-done.4 = s32[1,3,2,8]{3,2,1,0:T(2,128)S(1)} copy-done((s32[1,3,2,8]{3,2,1,0:T(2,128)S(1)}, s32[1,3,2,8]{3,2,1,0:T(2,128)}, u32[]{:S(2)}) %copy-start.4) | copy-done | bytes 216
  6.9 58.6 %relay.1 = (f32[16,64,128]{2,1,0:T(8,128)S(1)}, f32[16,64,128]{2,1,0:T(8,128)S(1)}) custom-call(s32[16,4]{1,0:T(8,128)S(1)} %copy.8.neighbors, s32[1,3,2,8]{3,2,1,0:T(2,128)S(1)} %copy-done.4, f32[16,64,128]{2,1,0:T(8,128)S(1)} %copy-done.2, f32[16,64,64]{2,1,0:T(8,128)S(1)} %copy-done.3, f32[16,4,64,64]{3,2,1,0:T(8,128)S(1)} %copy-done, ...), custom_call_target="tpu_custom_call" | custom-call | tf_op jit(solution)/shard_map/relay/pallas_call | solution.py:358
  65.5 0.8 %copy.11 = f32[16,64,128]{2,1,0:T(8,128)} copy(f32[16,64,128]{2,1,0:T(8,128)S(1)} %get-tuple-element.4) | data formatting | bytes 1048576
  66.3 0.8 %copy.12 = f32[16,64,128]{2,1,0:T(8,128)} copy(f32[16,64,128]{2,1,0:T(8,128)S(1)} %get-tuple-element.5) | data formatting | bytes 1048576
Async XLA Ops:
  1.4 1.6 %copy-start = (f32[16,4,64,64]{3,2,1,0:T(8,128)S(1)}, f32[16,4,64,64]{3,2,1,0:T(8,128)}, u32[]{:S(2)}) copy-start(f32[16,4,64,64]{3,2,1,0:T(8,128)} %nearby.1) | copy-start | bytes 3145732
  3.0 1.1 %copy-start.1 = (f32[1,3,8,64,64]{4,3,2,1,0:T(8,128)S(1)}, f32[1,3,8,64,64]{4,3,2,1,0:T(8,128)}, u32[]{:S(2)}) copy-start(f32[1,3,8,64,64]{4,3,2,1,0:T(8,128)} %remote.1) | copy-start | bytes 1179652
  4.1 1.0 %copy-start.2 = (f32[16,64,128]{2,1,0:T(8,128)S(1)}, f32[16,64,128]{2,1,0:T(8,128)}, u32[]{:S(2)}) copy-start(f32[16,64,128]{2,1,0:T(8,128)} %right_side.1) | copy-start | bytes 1572868
  5.2 1.0 %copy-start.3 = (f32[16,64,64]{2,1,0:T(8,128)S(1)}, f32[16,64,64]{2,1,0:T(8,128)}, u32[]{:S(2)}) copy-start(f32[16,64,64]{2,1,0:T(8,128)} %diagonal.1) | copy-start | bytes 786436
  6.2 0.7 %copy-start.4 = (s32[1,3,2,8]{3,2,1,0:T(2,128)S(1)}, s32[1,3,2,8]{3,2,1,0:T(2,128)}, u32[]{:S(2)}) copy-start(s32[1,3,2,8]{3,2,1,0:T(2,128)} %pairs.1) | copy-start | bytes 580

commit v2 on v1

--- a/solution.py
+++ b/solution.py
@@ -38,11 +38,12 @@
 
 def kernel(
     nx, nz,
+    neighbors_in, pairs_in, right_side_in, diagonal_in, nearby_in, remote_in,
+    solution, residual,
     neighbors, pairs, right_side, diagonal, nearby, remote,
-    solution, residual,
     w0, w1, z0, z1, r1, x_high, x_low, near_lhs, far_lhs, coupled,
     sent, received, first_sums, second_sums, inverse,
-    send_sem, recv_sem, first_send, first_recv, second_send, second_recv,
+    in_sem, send_sem, recv_sem, first_send, first_recv, second_send, second_recv,
 ):
     gx = lax.axis_index("gx")
     gy = lax.axis_index("gy")
@@ -66,9 +67,23 @@
             return carry
         return one
 
+    inputs = [
+        pltpu.make_async_copy(source, target, in_sem.at[n])
+        for n, (source, target) in enumerate(
+            (
+                (pairs_in, pairs),
+                (right_side_in, right_side),
+                (neighbors_in, neighbors),
+                (diagonal_in, diagonal),
+                (nearby_in, nearby),
+                (remote_in, remote),
+            )
+        )
+    ]
+    for copy in inputs:
+        copy.start()
     lax.fori_loop(1, n1, greet(first_peer), 0)
     lax.fori_loop(1, n2, greet(second_peer), 0)
-    pl.semaphore_wait(barrier, n1 + n2 - 2)
 
     bits = [(gy // (1 << e)) % 2 for e in range(CROSS)]
 
@@ -82,17 +97,25 @@
             device_id_type=MESH,
         )
 
-    def send_all(op, source):
+    def slot_of(half, q, e):
+        return q + (HALF * (1 - bits[e]) if half == 0 else HALF * bits[e])
+
+    def gather(op, half, q, block):
+        for e in LEVEL_ORDER:
+            t = slot_of(half, q, e)
+            sent[op, e, t] = block(jnp.maximum(pairs[0, e, 0, t], 0))
+
+    def send(op, half, q):
+        for e in LEVEL_ORDER:
+            slot_copy(op, e, slot_of(half, q, e)).start()
+
+    def send_all(op, block):
         for half in range(2):
             def one(q, carry):
-                for e in LEVEL_ORDER:
-                    base = HALF * (1 - bits[e]) if half == 0 else HALF * bits[e]
-                    t = base + q
-                    own = jnp.maximum(pairs[0, e, 0, t], 0)
-                    sent[op, e, t] = source[own]
-                    slot_copy(op, e, t).start()
+                gather(op, half, q, block)
+                send(op, half, q)
                 return carry
-            lax.fori_loop(0, HALF, one, 0)
+            lax.fori_loop(0, HALF, one, 0, unroll=2)
 
     def sum_copy(index, stage, k):
         buffer, sends, recvs, peer = (
@@ -142,42 +165,58 @@
         rows += [jnp.zeros((8 - len(rows), RHS), jnp.float32)] if len(rows) < 8 else []
         return jnp.concatenate(rows, axis=0)
 
-    def split_all(source):
-        def one(i, carry):
-            high, low = split(source[i])
-            x_high[i] = high
-            x_low[i] = low
-            return carry
-        lax.fori_loop(0, BLOCKS, one, 0)
+    def put(i, value):
+        high, low = split(value)
+        x_high[i] = high
+        x_low[i] = low
 
     def near_product(i):
-        sources = [i] + [jnp.bitwise_and(neighbors[i, k], BLOCKS - 1) for k in range(LOCAL)]
+        sources = [i] + [jnp.bitwise_and(neighbors[k, i], BLOCKS - 1) for k in range(LOCAL)]
         highs = [x_high[j] for j in sources]
         lows = [x_low[j] for j in sources]
         rhs = jnp.concatenate([h for high in highs for h in (high, high)] + lows, axis=0)
         return jnp.dot(near_lhs[i][:, : SOURCES * DEPTH], rhs, preferred_element_type=jnp.float32)
 
     def far_product(op, e, t):
-        slot_copy(op, e, t).wait_recv()
         high, low = split(received[op, e, t])
         rhs = jnp.concatenate([high, high, low], axis=0)
         product = jnp.dot(far_lhs[e, t][:, :DEPTH], rhs, preferred_element_type=jnp.float32)
         coupled[e, t] = product
         return product
 
+    def far_step(op, half, q):
+        slots = [slot_of(1 - half, q, e) for e in range(CROSS)]
+        for e in range(CROSS):
+            slot_copy(op, e, slots[e]).wait_recv()
+        return slots, [far_product(op, e, slots[e]) for e in range(CROSS)]
+
     def far_half(op, half):
         def one(q, carry):
-            for e in reversed(LEVEL_ORDER):
-                far_product(op, e, q + (HALF * bits[e] if half == 0 else HALF * (1 - bits[e])))
-            return carry
-        lax.fori_loop(0, HALF, one, 0)
-
-    def far_rows(i):
-        return [coupled[e, inverse[e * BLOCKS + i]] for e in range(CROSS)]
+            far_step(op, half, q)
+            return carry
+        lax.fori_loop(0, HALF, one, 0, unroll=2)
+
+    def join(near, i):
+        a, b, c = [coupled[e, inverse[e * BLOCKS + i]] for e in range(CROSS)]
+        return (near[i] + a) + (b + c)
 
     zero = jnp.zeros((8, RHS), jnp.float32)
 
-    send_all(0, right_side)
+    inputs[0].wait()
+    inputs[1].wait()
+    for half in range(2):
+        def prepare(q, carry):
+            gather(0, half, q, lambda j: right_side[j])
+            return carry
+        lax.fori_loop(0, HALF, prepare, 0)
+    pl.semaphore_wait(barrier, n1 + n2 - 2)
+    for half in range(2):
+        def begin(q, carry):
+            send(0, half, q)
+            return carry
+        lax.fori_loop(0, HALF, begin, 0)
+    for copy in inputs[2:]:
+        copy.wait()
 
     lane = lax.broadcasted_iota(jnp.int32, (WIDTH, 2 * WIDTH), 1)
 
@@ -195,7 +234,7 @@
             near_lhs[i, :, pl.ds((SOURCES * 2 + s) * WIDTH, 2 * WIDTH)] = pair.astype(jnp.bfloat16)
         return carry
 
-    lax.fori_loop(0, BLOCKS, near_setup, 0)
+    lax.fori_loop(0, BLOCKS, near_setup, 0, unroll=2)
 
     def far_setup(t, carry):
         for e in range(CROSS):
@@ -205,7 +244,7 @@
             far_lhs[e, t, :, pl.ds(2 * WIDTH, 2 * WIDTH)] = twice.astype(jnp.bfloat16)
         return carry
 
-    lax.fori_loop(0, SLOTS, far_setup, 0)
+    lax.fori_loop(0, SLOTS, far_setup, 0, unroll=2)
 
     for e in range(CROSS):
         coupled[e, SLOTS] = jnp.zeros((WIDTH, RHS), jnp.float32)
@@ -217,91 +256,88 @@
                 found = jnp.where(owns[t] == i, jnp.int32(t), found)
             inverse[e * BLOCKS + i] = found
             return carry
-        lax.fori_loop(0, BLOCKS, invert, 0)
-
-    split_all(right_side)
-
-    def w0_near(i, carry):
-        w0[i] = near_product(i)
-        return carry
-
-    lax.fori_loop(0, BLOCKS, w0_near, 0)
+        lax.fori_loop(0, BLOCKS, invert, 0, unroll=4)
+
+    def first_put(i, carry):
+        put(i, right_side[i])
+        return carry
+
+    lax.fori_loop(0, BLOCKS, first_put, 0, unroll=4)
+
+    def near_all(target):
+        def one(i, carry):
+            target[i] = near_product(i)
+            return carry
+        lax.fori_loop(0, BLOCKS, one, 0, unroll=4)
+
+    near_all(w0)
     far_half(0, 0)
     far_half(0, 1)
+
+    send_all(1, lambda j: join(w0, j))
 
     def w0_join(i, carry):
         gamma, delta = carry
         r = right_side[i]
-        w = w0[i] + tree_sum(far_rows(i) + [jnp.zeros_like(r)])
+        w = join(w0, i)
         w0[i] = w
+        put(i, w)
         return gamma + fold(r * r), delta + fold(w * r)
 
-    gamma, delta = lax.fori_loop(0, BLOCKS, w0_join, (zero, zero))
-
-    send_all(1, w0)
-    sum_start(0, 0, rows_of([gamma, delta]))
-    split_all(w0)
-
-    def z0_near(i, carry):
-        z0[i] = near_product(i)
-        return carry
-
-    lax.fori_loop(0, BLOCKS, z0_near, 0)
+    sums = lax.fori_loop(0, BLOCKS, w0_join, (zero, zero), unroll=4)
+    sum_start(0, 0, rows_of(sums))
+    near_all(z0)
     sum_start(0, 1, sum_finish(0, 0))
     far_half(1, 0)
-    far_half(1, 1)
     totals = sum_finish(0, 1)
     gamma0, delta0 = totals[0:1], totals[1:2]
     step0 = gamma0 / delta0
+    far_half(1, 1)
+
+    send_all(2, lambda j: w0[j] - step0 * join(z0, j))
 
     def z0_join(i, carry):
-        zz = z0[i] + tree_sum(far_rows(i) + [jnp.zeros((WIDTH, RHS), jnp.float32)])
+        zz, wa = join(z0, i), w0[i]
+        wb = wa - step0 * zz
+        r = right_side[i] - step0 * wa
         z0[i] = zz
-        w1[i] = w0[i] - step0 * zz
-        return carry
-
-    lax.fori_loop(0, BLOCKS, z0_join, 0)
-
-    send_all(2, w1)
-
-    def gram(i, carry):
-        wa, wb, zz = w0[i], w1[i], z0[i]
-        r = right_side[i] - step0 * wa
+        w1[i] = wb
         r1[i] = r
+        put(i, wb)
         terms = (r * r, r * wb, r * wa, wb * wb, wb * wa, wa * wa, wb * zz, wa * zz)
         return tuple(c + fold(t) for c, t in zip(carry, terms))
 
-    sums = lax.fori_loop(0, BLOCKS, gram, (zero,) * 8)
+    sums = lax.fori_loop(0, BLOCKS, z0_join, (zero,) * 8, unroll=2)
     sum_start(1, 0, rows_of(sums))
-    split_all(w1)
 
     def z1_near(i, energy):
         product = near_product(i)
         z1[i] = product
         return energy + fold(product * w1[i])
 
-    energy = lax.fori_loop(0, BLOCKS, z1_near, zero)
-
-    def energy_half(q, carry):
-        for e in reversed(LEVEL_ORDER):
-            t = q + HALF * bits[e]
-            product = far_product(2, e, t)
-            twice = jnp.where(pairs[0, e, 0, t] >= 0, 2.0 * fold(product * sent[2, e, t]), 0.0)
-            carry = carry + twice
-        return carry
-
-    energy = lax.fori_loop(0, HALF, energy_half, energy)
+    energy = lax.fori_loop(0, BLOCKS, z1_near, zero, unroll=4)
+    sum_start(1, 1, sum_finish(1, 0))
+
+    def energy_step(q, carry):
+        slots, products = far_step(2, 0, q)
+        for e in range(CROSS):
+            twice = 2.0 * fold(products[e] * sent[2, e, slots[e]])
+            carry = carry + jnp.where(pairs[0, e, 0, slots[e]] >= 0, twice, 0.0)
+        return carry
+
+    energy = lax.fori_loop(0, HALF, energy_step, energy, unroll=2)
     sum_start(2, 0, rows_of([energy]))
-    sum_start(1, 1, sum_finish(1, 0))
-    far_half(2, 1)
+    for q in range(HALF - 1):
+        far_step(2, 1, q)
     sum_start(2, 1, sum_finish(2, 0))
+    far_step(2, 1, HALF - 1)
     totals = sum_finish(1, 1)
     gamma1, delta1, rw0, w1w1, w1w0, w0w0, w1z0, w0z0 = [totals[k : k + 1] for k in range(8)]
     ratio1 = gamma1 / gamma0
     step1 = gamma1 / (delta1 - ratio1 * gamma1 / step0)
 
     def z1_join(i, carry):
-        zz = z1[i] + tree_sum(far_rows(i) + [jnp.zeros((WIDTH, RHS), jnp.float32)])
+        zz = join(z1, i)
         r, wa, wb, r0 = r1[i], w0[i], w1[i], right_side[i]
         p1 = r + ratio1 * r0
         ap1 = wb + ratio1 * wa
@@ -312,7 +348,7 @@
         w1[i] = ap1
         return carry
 
-    lax.fori_loop(0, BLOCKS, z1_join, 0)
+    lax.fori_loop(0, BLOCKS, z1_join, 0, unroll=4)
 
     w1aw1 = sum_finish(2, 1)[0:1]
     gamma2 = (
@@ -334,7 +370,7 @@
         residual[i] = r2 - step2 * (z1[i] + ratio2 * w1[i])
         return carry
 
-    lax.fori_loop(0, BLOCKS, last, 0)
+    lax.fori_loop(0, BLOCKS, last, 0, unroll=4)
 
     for op in range(3):
         def drain(t, carry):
@@ -353,14 +389,21 @@
     def local(right_side, diagonal_matrices, nearby_coupling_blocks, neighbors, pairs, remote_coupling_blocks):
         field = (BLOCKS, WIDTH, RHS)
         vmem = pl.BlockSpec(memory_space=pltpu.VMEM)
-        smem = pl.BlockSpec(memory_space=pltpu.SMEM)
         f32, bf16 = jnp.float32, jnp.bfloat16
         return pl.pallas_call(
             functools.partial(kernel, nx, nz),
             out_shape=(jax.ShapeDtypeStruct(field, f32), jax.ShapeDtypeStruct(field, f32)),
-            in_specs=[smem, smem, vmem, vmem, vmem, vmem],
+            in_specs=[pl.BlockSpec(memory_space=pl.ANY)] * 6,
             out_specs=(vmem, vmem),
-            scratch_shapes=[pltpu.VMEM(field, f32)] * 5
+            scratch_shapes=[
+                pltpu.SMEM((LOCAL, BLOCKS), jnp.int32),
+                pltpu.SMEM(pairs.shape, jnp.int32),
+                pltpu.VMEM(field, f32),
+                pltpu.VMEM(diagonal_matrices.shape, f32),
+                pltpu.VMEM(nearby_coupling_blocks.shape, f32),
+                pltpu.VMEM(remote_coupling_blocks.shape, f32),
+            ]
+            + [pltpu.VMEM(field, f32)] * 5
             + [
                 pltpu.VMEM(field, bf16),
                 pltpu.VMEM(field, bf16),
@@ -372,6 +415,7 @@
                 pltpu.VMEM((3, n1, 8, RHS), f32),
                 pltpu.VMEM((3, n2, 8, RHS), f32),
                 pltpu.SMEM((CROSS * BLOCKS,), jnp.int32),
+                pltpu.SemaphoreType.DMA((6,)),
                 pltpu.SemaphoreType.DMA((3, CROSS, SLOTS)),
                 pltpu.SemaphoreType.DMA((3, CROSS, SLOTS)),
                 pltpu.SemaphoreType.DMA((3,)),
@@ -380,10 +424,10 @@
                 pltpu.SemaphoreType.DMA((3,)),
             ],
             compiler_params=pltpu.CompilerParams(
-                collective_id=0, has_side_effects=True, vmem_limit_bytes=40 * 1024 * 1024
+                collective_id=0, has_side_effects=True, vmem_limit_bytes=56 * 1024 * 1024
             ),
             name="relay",
-        )(neighbors, pairs, right_side, diagonal_matrices, nearby_coupling_blocks, remote_coupling_blocks)
+        )(neighbors.T, pairs, right_side, diagonal_matrices, nearby_coupling_blocks, remote_coupling_blocks)
 
     wide = P(("gx", "gy"), None, None)
     return jax.shard_map(

time: 67.4 us -> 63.8 us (0.947)
  local copies, waits for them, and re-layouts: 7.84 us -> 3.77 us
    unnamed x13 -> x2, local copies, waits for them, and re-layouts: 7.84 us -> 3.77 us
where the time goes in v2:
time: 63.8 us; the launch traced here: 63.6 us
  Pallas kernels  59.2 us (93%)
  local copies, waits for them, and re-layouts  3.77 us (6%)
  between operations  0.64 us (1%)
    pallas_call x1, Pallas kernels, local(): pl.pallas_call(functools.partial(kernel, nx, nz), out_shape=(jax.ShapeDty...  59.2 us
    unnamed x2, local copies, waits for them, and re-layouts  3.77 us

profile of v2, /device:TPU:1, one launch (start us, length us, event | category | flops | bytes accessed | tf_op | source)
XLA Modules:
  0.0 63.6 jit_solution(13741899547061337862)
XLA Ops:
  0.6 59.2 %relay.1 = (f32[16,64,128]{2,1,0:T(8,128)}, f32[16,64,128]{2,1,0:T(8,128)}) custom-call(s32[4,16]{1,0:T(4,128)} %bitcast.1, s32[1,3,2,8]{3,2,1,0:T(2,128)} %pairs_in.1, f32[16,64,128]{2,1,0:T(8,128)} %right_side_in.1, f32[16,64,64]{2,1,0:T(8,128)} %diagonal_in.1, f32[16,4,64,64]{3,2,1,0:T(8,128)} %nearby_in.1, f32[1,3,8,64,64]{4,3,2,1,0:T(8,128)} %remote_in.1), custom_call_target="tpu_custom_call" | custom-call | tf_op jit(solution)/shard_map/relay/pallas_call | solution.py:393
  59.8 1.9 %copy.10 = f32[16,64,128]{2,1,0:T(8,128)} copy(f32[16,64,128]{2,1,0:T(8,128)} %get-tuple-element.4) | data formatting | bytes 1048576
  61.7 1.9 %copy.11 = f32[16,64,128]{2,1,0:T(8,128)} copy(f32[16,64,128]{2,1,0:T(8,128)} %get-tuple-element.5) | data formatting | bytes 1048576

commit v3 on v2

--- a/solution.py
+++ b/solution.py
@@ -39,7 +39,7 @@
 def kernel(
     nx, nz,
     neighbors_in, pairs_in, right_side_in, diagonal_in, nearby_in, remote_in,
-    solution, residual,
+    so_far, residual, direction, image, dir_image, last_steps,
     neighbors, pairs, right_side, diagonal, nearby, remote,
     w0, w1, z0, z1, r1, x_high, x_low, near_lhs, far_lhs, coupled,
     sent, received, first_sums, second_sums, inverse,
@@ -47,17 +47,17 @@
 ):
     gx = lax.axis_index("gx")
     gy = lax.axis_index("gy")
-    z, y, core = gy // 8, (gy // 2) % 4, gy % 2
-    n1, n2 = 2 * nz, 4 * nx
-    me1, me2 = z * 2 + core, gx * 4 + y
+    z, y, core = gy >> 3, (gy >> 1) & 3, gy & 1
+    n1, n2 = 4 * nx, 2 * nz
+    me1, me2 = gx * 4 + y, z * 2 + core
 
     def first_peer(k):
         other = jnp.bitwise_xor(me1, k)
-        return gx, ((other // 2) * 4 + y) * 2 + other % 2
+        return other >> 2, (z << 3) + ((other & 3) << 1) + core
 
     def second_peer(k):
         other = jnp.bitwise_xor(me2, k)
-        return other // 4, (z * 4 + other % 4) * 2 + core
+        return gx, ((other >> 1) << 3) + (y << 1) + (other & 1)
 
     barrier = pltpu.get_barrier_semaphore()
 
@@ -109,13 +109,12 @@
         for e in LEVEL_ORDER:
             slot_copy(op, e, slot_of(half, q, e)).start()
 
-    def send_all(op, block):
-        for half in range(2):
-            def one(q, carry):
-                gather(op, half, q, block)
-                send(op, half, q)
-                return carry
-            lax.fori_loop(0, HALF, one, 0, unroll=2)
+    def send_half(op, half, block):
+        def one(q, carry):
+            gather(op, half, q, block)
+            send(op, half, q)
+            return carry
+        lax.fori_loop(0, HALF, one, 0, unroll=2)
 
     def sum_copy(index, stage, k):
         buffer, sends, recvs, peer = (
@@ -196,6 +195,23 @@
             return carry
         lax.fori_loop(0, HALF, one, 0, unroll=2)
 
+    def energy_half(op, source, energy):
+        def one(q, carry):
+            slots, products = far_step(op, 0, q)
+            for e in range(CROSS):
+                own = pairs[0, e, 0, slots[e]]
+                twice = 2.0 * fold(products[e] * source[jnp.maximum(own, 0)])
+                carry = carry + jnp.where(own >= 0, twice, 0.0)
+            return carry
+        return lax.fori_loop(0, HALF, one, energy, unroll=2)
+
+    def near_energy(target, source):
+        def one(i, energy):
+            product = near_product(i)
+            target[i] = product
+            return energy + fold(product * source[i])
+        return lax.fori_loop(0, BLOCKS, one, zero, unroll=4)
+
     def join(near, i):
         a, b, c = [coupled[e, inverse[e * BLOCKS + i]] for e in range(CROSS)]
         return (near[i] + a) + (b + c)
@@ -258,11 +274,12 @@
             return carry
         lax.fori_loop(0, BLOCKS, invert, 0, unroll=4)
 
-    def first_put(i, carry):
-        put(i, right_side[i])
-        return carry
-
-    lax.fori_loop(0, BLOCKS, first_put, 0, unroll=4)
+    def first_put(i, gamma):
+        r = right_side[i]
+        put(i, r)
+        return gamma + fold(r * r)
+
+    gamma = lax.fori_loop(0, BLOCKS, first_put, zero, unroll=4)
 
     def near_all(target):
         def one(i, carry):
@@ -270,31 +287,29 @@
             return carry
         lax.fori_loop(0, BLOCKS, one, 0, unroll=4)
 
-    near_all(w0)
-    far_half(0, 0)
+    energy = energy_half(0, right_side, near_energy(w0, right_side))
+    sum_start(0, 0, rows_of([gamma, energy]))
     far_half(0, 1)
 
-    send_all(1, lambda j: join(w0, j))
+    for half in range(2):
+        send_half(1, half, lambda j: join(w0, j))
 
     def w0_join(i, carry):
-        gamma, delta = carry
-        r = right_side[i]
         w = join(w0, i)
         w0[i] = w
         put(i, w)
-        return gamma + fold(r * r), delta + fold(w * r)
-
-    sums = lax.fori_loop(0, BLOCKS, w0_join, (zero, zero), unroll=4)
-    sum_start(0, 0, rows_of(sums))
+        return carry
+
+    lax.fori_loop(0, BLOCKS, w0_join, 0, unroll=4)
+    sum_start(0, 1, sum_finish(0, 0))
     near_all(z0)
-    sum_start(0, 1, sum_finish(0, 0))
     far_half(1, 0)
     totals = sum_finish(0, 1)
     gamma0, delta0 = totals[0:1], totals[1:2]
     step0 = gamma0 / delta0
     far_half(1, 1)
 
-    send_all(2, lambda j: w0[j] - step0 * join(z0, j))
+    send_half(2, 0, lambda j: w0[j] - step0 * join(z0, j))
 
     def z0_join(i, carry):
         zz, wa = join(z0, i), w0[i]
@@ -310,27 +325,13 @@
     sums = lax.fori_loop(0, BLOCKS, z0_join, (zero,) * 8, unroll=2)
     sum_start(1, 0, rows_of(sums))
 
-    def z1_near(i, energy):
-        product = near_product(i)
-        z1[i] = product
-        return energy + fold(product * w1[i])
-
-    energy = lax.fori_loop(0, BLOCKS, z1_near, zero, unroll=4)
+    energy = near_energy(z1, w1)
     sum_start(1, 1, sum_finish(1, 0))
-
-    def energy_step(q, carry):
-        slots, products = far_step(2, 0, q)
-        for e in range(CROSS):
-            twice = 2.0 * fold(products[e] * sent[2, e, slots[e]])
-            carry = carry + jnp.where(pairs[0, e, 0, slots[e]] >= 0, twice, 0.0)
-        return carry
-
-    energy = lax.fori_loop(0, HALF, energy_step, energy, unroll=2)
+    energy = energy_half(2, w1, energy)
     sum_start(2, 0, rows_of([energy]))
-    for q in range(HALF - 1):
-        far_step(2, 1, q)
+    send_half(2, 1, lambda j: w1[j])
     sum_start(2, 1, sum_finish(2, 0))
-    far_step(2, 1, HALF - 1)
+    far_half(2, 1)
     totals = sum_finish(1, 1)
     gamma1, delta1, rw0, w1w1, w1w0, w0w0, w1z0, w0z0 = [totals[k : k + 1] for k in range(8)]
     ratio1 = gamma1 / gamma0
@@ -341,11 +342,11 @@
         r, wa, wb, r0 = r1[i], w0[i], w1[i], right_side[i]
         p1 = r + ratio1 * r0
         ap1 = wb + ratio1 * wa
-        solution[i] = step0 * r0 + step1 * p1
+        so_far[i] = step0 * r0 + step1 * p1
         residual[i] = r - step1 * ap1
-        z1[i] = wb - step1 * (zz + ratio1 * z0[i])
-        r1[i] = p1
-        w1[i] = ap1
+        image[i] = wb - step1 * (zz + ratio1 * z0[i])
+        direction[i] = p1
+        dir_image[i] = ap1
         return carry
 
     lax.fori_loop(0, BLOCKS, z1_join, 0, unroll=4)
@@ -364,13 +365,7 @@
     ratio2 = gamma2 / gamma1
     step2 = gamma2 / (delta2 - ratio2 * gamma2 / step1)
 
-    def last(i, carry):
-        r2 = residual[i]
-        solution[i] = solution[i] + step2 * (r2 + ratio2 * r1[i])
-        residual[i] = r2 - step2 * (z1[i] + ratio2 * w1[i])
-        return carry
-
-    lax.fori_loop(0, BLOCKS, last, 0, unroll=4)
+    last_steps[...] = jnp.concatenate([step2, step2 * ratio2, jnp.zeros((6, RHS), jnp.float32)], axis=0)
 
     for op in range(3):
         def drain(t, carry):
@@ -384,17 +379,17 @@
 
 def solution(mesh):
     nx, nz = mesh.shape["gx"], mesh.shape["gy"] // 8
-    n1, n2 = 2 * nz, 4 * nx
+    n1, n2 = 4 * nx, 2 * nz
 
     def local(right_side, diagonal_matrices, nearby_coupling_blocks, neighbors, pairs, remote_coupling_blocks):
         field = (BLOCKS, WIDTH, RHS)
         vmem = pl.BlockSpec(memory_space=pltpu.VMEM)
         f32, bf16 = jnp.float32, jnp.bfloat16
-        return pl.pallas_call(
+        so_far, residual, direction, image, dir_image, last_steps = pl.pallas_call(
             functools.partial(kernel, nx, nz),
-            out_shape=(jax.ShapeDtypeStruct(field, f32), jax.ShapeDtypeStruct(field, f32)),
+            out_shape=(jax.ShapeDtypeStruct(field, f32),) * 5 + (jax.ShapeDtypeStruct((8, RHS), f32),),
             in_specs=[pl.BlockSpec(memory_space=pl.ANY)] * 6,
-            out_specs=(vmem, vmem),
+            out_specs=(vmem,) * 6,
             scratch_shapes=[
                 pltpu.SMEM((LOCAL, BLOCKS), jnp.int32),
                 pltpu.SMEM(pairs.shape, jnp.int32),
@@ -424,10 +419,14 @@
                 pltpu.SemaphoreType.DMA((3,)),
             ],
             compiler_params=pltpu.CompilerParams(
-                collective_id=0, has_side_effects=True, vmem_limit_bytes=56 * 1024 * 1024
+                collective_id=0, has_side_effects=True, vmem_limit_bytes=52 * 1024 * 1024
             ),
             name="relay",
         )(neighbors.T, pairs, right_side, diagonal_matrices, nearby_coupling_blocks, remote_coupling_blocks)
+        step, shared = last_steps[0], last_steps[1]
+        solution = so_far + (step * residual + shared * direction)
+        residual = residual - (step * image + shared * dir_image)
+        return solution, residual
 
     wide = P(("gx", "gy"), None, None)
     return jax.shard_map(

time: 63.8 us -> 62.8 us (0.984)
  other arithmetic: 0 us -> 2.41 us
  local copies, waits for them, and re-layouts: 3.77 us -> 1.36 us
  Pallas kernels: 59.2 us -> 58.2 us
    sub x0 -> x1, other arithmetic: none -> 2.41 us  [local(): residual = residual - (step * image + shared * dir_image)]
    unnamed x2 -> x4, local copies, waits for them, and re-layouts: 3.77 us -> 1.36 us
    pallas_call x1, Pallas kernels: 59.2 us -> 58.2 us  [local(): pl.pallas_call(functools.partial(kernel, nx, nz), out_shape=(jax.ShapeDty...]
where the time goes in v3:
time: 62.8 us; the launch traced here: 62.6 us
  Pallas kernels  58.2 us (93%)
  other arithmetic  2.41 us (4%)
  local copies, waits for them, and re-layouts  1.36 us (2%)
  between operations  0.66 us (1%)
    pallas_call x1, Pallas kernels, local(): pl.pallas_call(functools.partial(kernel, nx, nz), out_shape=(jax.ShapeDty...  58.2 us
    sub x1, other arithmetic, local(): residual = residual - (step * image + shared * dir_image)  2.41 us
    unnamed x4, local copies, waits for them, and re-layouts  1.36 us

profile of v3, /device:TPU:1, one launch (start us, length us, event | category | flops | bytes accessed | tf_op | source)
XLA Modules:
  0.0 62.6 jit_solution(16731786732689345143)
XLA Ops:
  0.6 0.0 copy-start
  0.6 0.7 %copy-done = s32[1,3,2,8]{3,2,1,0:T(2,128)S(1)} copy-done((s32[1,3,2,8]{3,2,1,0:T(2,128)S(1)}, s32[1,3,2,8]{3,2,1,0:T(2,128)}, u32[]{:S(2)}) %copy-start) | copy-done | bytes 216
  1.3 0.0 copy-start.1
  1.3 0.7 %copy-done.1 = s32[16,4]{0,1:T(4,128)S(1)} copy-done((s32[16,4]{0,1:T(4,128)S(1)}, s32[16,4]{0,1:T(4,128)}, u32[]{:S(2)}) %copy-start.1) | copy-done | bytes 280
  2.0 58.2 %relay.1 = (f32[16,64,128]{2,1,0:T(8,128)S(1)}, f32[16,64,128]{2,1,0:T(8,128)S(1)}, f32[16,64,128]{2,1,0:T(8,128)S(1)}, f32[16,64,128]{2,1,0:T(8,128)}, f32[16,64,128]{2,1,0:T(8,128)}, /*index=5*/f32[8,128]{1,0:T(8,128)S(1)}) custom-call(s32[4,16]{1,0:T(4,128)S(1)} %bitcast.5, s32[1,3,2,8]{3,2,1,0:T(2,128)S(1)} %copy-done, f32[16,64,128]{2,1,0:T(8,128)} %right_side_in.1, ...), custom_call_target="tpu_custom_call" | custom-call | tf_op jit(solution)/shard_map/relay/pallas_call | solution.py:388
  60.2 2.4 %add_subtract_fusion = (f32[16,64,128]{2,1,0:T(8,128)}, f32[16,64,128]{2,1,0:T(8,128)}) fusion(f32[16,64,128]{2,1,0:T(8,128)S(1)} %get-tuple-element.10, f32[16,64,128]{2,1,0:T(8,128)} %get-tuple-element.13, f32[16,64,128]{2,1,0:T(8,128)} %get-tuple-element.12, f32[128]{0:T(128)S(1)} %get-tuple-element.17, f32[128]{0:T(128)S(1)} %get-tuple-element.16, ...), kind=kLoop, calls=%fused_computation | loop fusion | flops 1048576 | bytes 3671040 | tf_op jit(solution)/shard_map/sub | solution.py:428
  (1 shorter events, 0.0 us)
Async XLA Ops:
  0.6 0.7 %copy-start = (s32[1,3,2,8]{3,2,1,0:T(2,128)S(1)}, s32[1,3,2,8]{3,2,1,0:T(2,128)}, u32[]{:S(2)}) copy-start(s32[1,3,2,8]{3,2,1,0:T(2,128)} %pairs_in.1) | copy-start | bytes 580
  1.3 0.7 %copy-start.1 = (s32[16,4]{0,1:T(4,128)S(1)}, s32[16,4]{0,1:T(4,128)}, u32[]{:S(2)}) copy-start(s32[16,4]{0,1:T(4,128)} %param.9) | copy-start | bytes 772

commit v4 on v3

--- a/solution.py
+++ b/solution.py
@@ -39,9 +39,9 @@
 def kernel(
     nx, nz,
     neighbors_in, pairs_in, right_side_in, diagonal_in, nearby_in, remote_in,
-    so_far, residual, direction, image, dir_image, last_steps,
+    w0, w1, z0, z1, factors,
     neighbors, pairs, right_side, diagonal, nearby, remote,
-    w0, w1, z0, z1, r1, x_high, x_low, near_lhs, far_lhs, coupled,
+    x_high, x_low, near_lhs, far_lhs, coupled,
     sent, received, first_sums, second_sums, inverse,
     in_sem, send_sem, recv_sem, first_send, first_recv, second_send, second_recv,
 ):
@@ -80,7 +80,7 @@
             )
         )
     ]
-    for copy in inputs:
+    for copy in inputs[:2]:
         copy.start()
     lax.fori_loop(1, n1, greet(first_peer), 0)
     lax.fori_loop(1, n2, greet(second_peer), 0)
@@ -149,10 +149,8 @@
         buffer, n = ((first_sums, n1), (second_sums, n2))[stage]
         buffer[index, 0] = value
 
-        def one(k, carry):
+        for k in range(n - 1, 0, -1):
             sum_copy(index, stage, k).start()
-            return carry
-        lax.fori_loop(1, n, one, 0)
 
     def sum_finish(index, stage):
         buffer, n = ((first_sums, n1), (second_sums, n2))[stage]
@@ -220,6 +218,8 @@
 
     inputs[0].wait()
     inputs[1].wait()
+    for copy in inputs[2:]:
+        copy.start()
     for half in range(2):
         def prepare(q, carry):
             gather(0, half, q, lambda j: right_side[j])
@@ -317,41 +317,27 @@
         r = right_side[i] - step0 * wa
         z0[i] = zz
         w1[i] = wb
-        r1[i] = r
         put(i, wb)
-        terms = (r * r, r * wb, r * wa, wb * wb, wb * wa, wa * wa, wb * zz, wa * zz)
+        terms = (r * r, r * wb, wb * wb, wb * wa, wa * wa, wb * zz, wa * zz)
         return tuple(c + fold(t) for c, t in zip(carry, terms))
 
-    sums = lax.fori_loop(0, BLOCKS, z0_join, (zero,) * 8, unroll=2)
-    sum_start(1, 0, rows_of(sums))
-
-    energy = near_energy(z1, w1)
+    sums = lax.fori_loop(0, BLOCKS, z0_join, (zero,) * 7, unroll=2)
+    energy = energy_half(2, w1, near_energy(z1, w1))
+    sum_start(1, 0, rows_of(list(sums) + [energy]))
+    send_half(2, 1, lambda j: w1[j])
     sum_start(1, 1, sum_finish(1, 0))
-    energy = energy_half(2, w1, energy)
-    sum_start(2, 0, rows_of([energy]))
-    send_half(2, 1, lambda j: w1[j])
-    sum_start(2, 1, sum_finish(2, 0))
     far_half(2, 1)
+
+    def z1_join(i, carry):
+        z1[i] = join(z1, i)
+        return carry
+
+    lax.fori_loop(0, BLOCKS, z1_join, 0, unroll=4)
     totals = sum_finish(1, 1)
-    gamma1, delta1, rw0, w1w1, w1w0, w0w0, w1z0, w0z0 = [totals[k : k + 1] for k in range(8)]
+    gamma1, delta1, w1w1, w1w0, w0w0, w1z0, w0z0, w1aw1 = [totals[k : k + 1] for k in range(8)]
+    rw0 = delta0 - step0 * w0w0
     ratio1 = gamma1 / gamma0
     step1 = gamma1 / (delta1 - ratio1 * gamma1 / step0)
-
-    def z1_join(i, carry):
-        zz = join(z1, i)
-        r, wa, wb, r0 = r1[i], w0[i], w1[i], right_side[i]
-        p1 = r + ratio1 * r0
-        ap1 = wb + ratio1 * wa
-        so_far[i] = step0 * r0 + step1 * p1
-        residual[i] = r - step1 * ap1
-        image[i] = wb - step1 * (zz + ratio1 * z0[i])
-        direction[i] = p1
-        dir_image[i] = ap1
-        return carry
-
-    lax.fori_loop(0, BLOCKS, z1_join, 0, unroll=4)
-
-    w1aw1 = sum_finish(2, 1)[0:1]
     gamma2 = (
         gamma1
         - 2.0 * step1 * (delta1 + ratio1 * rw0)
@@ -364,8 +350,19 @@
     )
     ratio2 = gamma2 / gamma1
     step2 = gamma2 / (delta2 - ratio2 * gamma2 / step1)
-
-    last_steps[...] = jnp.concatenate([step2, step2 * ratio2, jnp.zeros((6, RHS), jnp.float32)], axis=0)
+    both_steps = step1 * step2
+    factors[...] = jnp.concatenate(
+        [
+            step0 + step1 * (1.0 + ratio1) + step2 * (1.0 + ratio2 * (1.0 + ratio1)),
+            step0 * (step1 + step2 * (1.0 + ratio2)) + both_steps * ratio1,
+            both_steps,
+            step0 + ratio1 * (step1 + step2 * ratio2),
+            step1 + step2 * (1.0 + ratio2),
+            both_steps * ratio1,
+            jnp.zeros((2, RHS), jnp.float32),
+        ],
+        axis=0,
+    )
 
     for op in range(3):
         def drain(t, carry):
@@ -373,8 +370,9 @@
                 slot_copy(op, e, t).wait_send()
             return carry
         lax.fori_loop(0, SLOTS, drain, 0)
+    for index in range(2):
         for stage in range(2):
-            sum_all_wait(op, stage).wait_send()
+            sum_all_wait(index, stage).wait_send()
 
 
 def solution(mesh):
@@ -385,11 +383,11 @@
         field = (BLOCKS, WIDTH, RHS)
         vmem = pl.BlockSpec(memory_space=pltpu.VMEM)
         f32, bf16 = jnp.float32, jnp.bfloat16
-        so_far, residual, direction, image, dir_image, last_steps = pl.pallas_call(
+        w0, w1, z0, z1, factors = pl.pallas_call(
             functools.partial(kernel, nx, nz),
-            out_shape=(jax.ShapeDtypeStruct(field, f32),) * 5 + (jax.ShapeDtypeStruct((8, RHS), f32),),
+            out_shape=(jax.ShapeDtypeStruct(field, f32),) * 4 + (jax.ShapeDtypeStruct((8, RHS), f32),),
             in_specs=[pl.BlockSpec(memory_space=pl.ANY)] * 6,
-            out_specs=(vmem,) * 6,
+            out_specs=(vmem,) * 5,
             scratch_shapes=[
                 pltpu.SMEM((LOCAL, BLOCKS), jnp.int32),
                 pltpu.SMEM(pairs.shape, jnp.int32),
@@ -398,7 +396,6 @@
                 pltpu.VMEM(nearby_coupling_blocks.shape, f32),
                 pltpu.VMEM(remote_coupling_blocks.shape, f32),
             ]
-            + [pltpu.VMEM(field, f32)] * 5
             + [
                 pltpu.VMEM(field, bf16),
                 pltpu.VMEM(field, bf16),
@@ -407,25 +404,24 @@
                 pltpu.VMEM((CROSS, SLOTS + 1, WIDTH, RHS), f32),
                 pltpu.VMEM((3, CROSS, SLOTS, WIDTH, RHS), f32),
                 pltpu.VMEM((3, CROSS, SLOTS, WIDTH, RHS), f32),
-                pltpu.VMEM((3, n1, 8, RHS), f32),
-                pltpu.VMEM((3, n2, 8, RHS), f32),
+                pltpu.VMEM((2, n1, 8, RHS), f32),
+                pltpu.VMEM((2, n2, 8, RHS), f32),
                 pltpu.SMEM((CROSS * BLOCKS,), jnp.int32),
                 pltpu.SemaphoreType.DMA((6,)),
                 pltpu.SemaphoreType.DMA((3, CROSS, SLOTS)),
                 pltpu.SemaphoreType.DMA((3, CROSS, SLOTS)),
-                pltpu.SemaphoreType.DMA((3,)),
-                pltpu.SemaphoreType.DMA((3,)),
-                pltpu.SemaphoreType.DMA((3,)),
-                pltpu.SemaphoreType.DMA((3,)),
+                pltpu.SemaphoreType.DMA((2,)),
+                pltpu.SemaphoreType.DMA((2,)),
+                pltpu.SemaphoreType.DMA((2,)),
+                pltpu.SemaphoreType.DMA((2,)),
             ],
             compiler_params=pltpu.CompilerParams(
-                collective_id=0, has_side_effects=True, vmem_limit_bytes=52 * 1024 * 1024
+                collective_id=0, has_side_effects=True, vmem_limit_bytes=51 * 1024 * 1024
             ),
             name="relay",
         )(neighbors.T, pairs, right_side, diagonal_matrices, nearby_coupling_blocks, remote_coupling_blocks)
-        step, shared = last_steps[0], last_steps[1]
-        solution = so_far + (step * residual + shared * direction)
-        residual = residual - (step * image + shared * dir_image)
+        solution = (factors[0] * right_side - factors[1] * w0) - factors[2] * w1
+        residual = ((right_side - factors[3] * w0) - factors[4] * w1) + (factors[5] * z0 + factors[2] * z1)
         return solution, residual
 
     wide = P(("gx", "gy"), None, None)

time: 62.8 us -> 59.7 us (0.951)
  Pallas kernels: 58.2 us -> 55.2 us
  other arithmetic: 2.41 us -> 1.26 us
  local copies, waits for them, and re-layouts: 1.36 us -> 2.41 us
    pallas_call x1, Pallas kernels: 58.2 us -> 55.2 us  [local(): pl.pallas_call(functools.partial(kernel, nx, nz), out_shape=(jax.ShapeDty...]
    sub x1 -> x0, other arithmetic: 2.41 us -> none  [local(): residual = residual - (step * image + shared * dir_image)]
    add x0 -> x1, other arithmetic: none -> 1.26 us  [local(): right_side - factors[3] * w0 - factors[4] * w1 + (factors[5] * z0 + facto...]
    unnamed x4 -> x6, local copies, waits for them, and re-layouts: 1.36 us -> 2.4 us
where the time goes in v4:
time: 59.7 us; the launch traced here: 59.5 us
  Pallas kernels  55.2 us (92%)
  local copies, waits for them, and re-layouts  2.41 us (4%)
  other arithmetic  1.26 us (2%)
  between operations  0.66 us (1%)
    pallas_call x1, Pallas kernels, local(): pl.pallas_call(functools.partial(kernel, nx, nz), out_shape=(jax.ShapeDty...  55.2 us
    unnamed x6, local copies, waits for them, and re-layouts  2.4 us
    add x1, other arithmetic, local(): right_side - factors[3] * w0 - factors[4] * w1 + (factors[5] * z0 + facto...  1.26 us

profile of v4, /device:TPU:1, one launch (start us, length us, event | category | flops | bytes accessed | tf_op | source)
XLA Modules:
  0.0 59.5 jit_solution(2262191886655247218)
XLA Ops:
  0.6 0.0 copy-start
  0.6 1.0 %copy-done = f32[16,64,128]{2,1,0:T(8,128)S(1)} copy-done((f32[16,64,128]{2,1,0:T(8,128)S(1)}, f32[16,64,128]{2,1,0:T(8,128)}, u32[]{:S(2)}) %copy-start) | copy-done | bytes 524312
  1.7 0.0 copy-start.1
  1.7 0.7 %copy-done.1 = s32[1,3,2,8]{3,2,1,0:T(2,128)S(1)} copy-done((s32[1,3,2,8]{3,2,1,0:T(2,128)S(1)}, s32[1,3,2,8]{3,2,1,0:T(2,128)}, u32[]{:S(2)}) %copy-start.1) | copy-done | bytes 216
  2.4 0.0 copy-start.2
  2.4 0.7 %copy-done.2 = s32[16,4]{0,1:T(4,128)S(1)} copy-done((s32[16,4]{0,1:T(4,128)S(1)}, s32[16,4]{0,1:T(4,128)}, u32[]{:S(2)}) %copy-start.2) | copy-done | bytes 280
  3.0 55.2 %relay.1 = (f32[16,64,128]{2,1,0:T(8,128)S(1)}, f32[16,64,128]{2,1,0:T(8,128)S(1)}, f32[16,64,128]{2,1,0:T(8,128)S(1)}, f32[16,64,128]{2,1,0:T(8,128)S(1)}, f32[8,128]{1,0:T(8,128)S(1)}) custom-call(s32[4,16]{1,0:T(4,128)S(1)} %bitcast.13, s32[1,3,2,8]{3,2,1,0:T(2,128)S(1)} %copy-done.1, f32[16,64,128]{2,1,0:T(8,128)S(1)} %copy-done, ...), custom_call_target="tpu_custom_call" | custom-call | tf_op jit(solution)/shard_map/relay/pallas_call | solution.py:386
  58.3 1.3 %add_add_fusion = (f32[16,64,128]{2,1,0:T(8,128)}, f32[16,64,128]{2,1,0:T(8,128)}) fusion(f32[16,64,128]{2,1,0:T(8,128)S(1)} %get-tuple-element.11, f32[16,64,128]{2,1,0:T(8,128)S(1)} %get-tuple-element.10, f32[16,64,128]{2,1,0:T(8,128)S(1)} %get-tuple-element.9, f32[16,64,128]{2,1,0:T(8,128)S(1)} %copy-done, f32[16,64,128]{2,1,0:T(8,128)S(1)} %get-tuple-element.8, ...), kind=kLoop, calls=%fused_computation | loop fusion | flops 1703936 | bytes 3673088 | tf_op jit(solution)/shard_map/add | solution.py:424
  (1 shorter events, 0.0 us)
Async XLA Ops:
  0.6 1.0 %copy-start = (f32[16,64,128]{2,1,0:T(8,128)S(1)}, f32[16,64,128]{2,1,0:T(8,128)}, u32[]{:S(2)}) copy-start(f32[16,64,128]{2,1,0:T(8,128)} %right_side_in.1) | copy-start | bytes 1572868
  1.7 0.7 %copy-start.1 = (s32[1,3,2,8]{3,2,1,0:T(2,128)S(1)}, s32[1,3,2,8]{3,2,1,0:T(2,128)}, u32[]{:S(2)}) copy-start(s32[1,3,2,8]{3,2,1,0:T(2,128)} %pairs_in.1) | copy-start | bytes 580
  2.4 0.7 %copy-start.2 = (s32[16,4]{0,1:T(4,128)S(1)}, s32[16,4]{0,1:T(4,128)}, u32[]{:S(2)}) copy-start(s32[16,4]{0,1:T(4,128)} %param.9) | copy-start | bytes 772

commit v5 on v4

--- a/solution.py
+++ b/solution.py
@@ -15,7 +15,7 @@
 WIDTH = 64
 RHS = 128
 SOURCES = LOCAL + 1
-DEPTH = 3 * WIDTH
+DEPTH = 4 * WIDTH
 MESH = pl.DeviceIdType.MESH
 LEVEL_ORDER = (2, 1, 0)
 
@@ -27,9 +27,21 @@
 
 
 def split(value):
-    high = value.astype(jnp.bfloat16)
-    low = (value - high.astype(jnp.float32)).astype(jnp.bfloat16)
-    return high, low
+    parts = []
+    for _ in range(3):
+        parts.append(value.astype(jnp.bfloat16))
+        value = value - parts[-1].astype(jnp.float32)
+    return parts
+
+
+def product(tiles, parts):
+    lhs, rhs = [], []
+    for tile, (high, mid, low) in zip(tiles, parts):
+        lhs += [tile[:, : 2 * WIDTH], tile]
+        rhs += [high, high, mid, mid, low, high]
+    return jnp.dot(
+        jnp.concatenate(lhs, axis=1), jnp.concatenate(rhs, axis=0), preferred_element_type=jnp.float32
+    )
 
 
 def fold(value):
@@ -41,7 +53,7 @@
     neighbors_in, pairs_in, right_side_in, diagonal_in, nearby_in, remote_in,
     w0, w1, z0, z1, factors,
     neighbors, pairs, right_side, diagonal, nearby, remote,
-    x_high, x_low, near_lhs, far_lhs, coupled,
+    x_high, x_mid, x_low, near_lhs, far_lhs, coupled,
     sent, received, first_sums, second_sums, inverse,
     in_sem, send_sem, recv_sem, first_send, first_recv, second_send, second_recv,
 ):
@@ -114,7 +126,7 @@
             gather(op, half, q, block)
             send(op, half, q)
             return carry
-        lax.fori_loop(0, HALF, one, 0, unroll=2)
+        lax.fori_loop(0, HALF, one, 0, unroll=4)
 
     def sum_copy(index, stage, k):
         buffer, sends, recvs, peer = (
@@ -163,23 +175,18 @@
         return jnp.concatenate(rows, axis=0)
 
     def put(i, value):
-        high, low = split(value)
-        x_high[i] = high
-        x_low[i] = low
+        for store, part in zip((x_high, x_mid, x_low), split(value)):
+            store[i] = part
 
     def near_product(i):
         sources = [i] + [jnp.bitwise_and(neighbors[k, i], BLOCKS - 1) for k in range(LOCAL)]
-        highs = [x_high[j] for j in sources]
-        lows = [x_low[j] for j in sources]
-        rhs = jnp.concatenate([h for high in highs for h in (high, high)] + lows, axis=0)
-        return jnp.dot(near_lhs[i][:, : SOURCES * DEPTH], rhs, preferred_element_type=jnp.float32)
+        parts = [(x_high[j], x_mid[j], x_low[j]) for j in sources]
+        return product([near_lhs[i, s] for s in range(SOURCES)], parts)
 
     def far_product(op, e, t):
-        high, low = split(received[op, e, t])
-        rhs = jnp.concatenate([high, high, low], axis=0)
-        product = jnp.dot(far_lhs[e, t][:, :DEPTH], rhs, preferred_element_type=jnp.float32)
-        coupled[e, t] = product
-        return product
+        result = product([far_lhs[e, t]], [split(received[op, e, t])])
+        coupled[e, t] = result
+        return result
 
     def far_step(op, half, q):
         slots = [slot_of(1 - half, q, e) for e in range(CROSS)]
@@ -191,7 +198,7 @@
         def one(q, carry):
             far_step(op, half, q)
             return carry
-        lax.fori_loop(0, HALF, one, 0, unroll=2)
+        lax.fori_loop(0, HALF, one, 0, unroll=4)
 
     def energy_half(op, source, energy):
         def one(q, carry):
@@ -201,13 +208,13 @@
                 twice = 2.0 * fold(products[e] * source[jnp.maximum(own, 0)])
                 carry = carry + jnp.where(own >= 0, twice, 0.0)
             return carry
-        return lax.fori_loop(0, HALF, one, energy, unroll=2)
+        return lax.fori_loop(0, HALF, one, energy, unroll=4)
 
     def near_energy(target, source):
         def one(i, energy):
-            product = near_product(i)
-            target[i] = product
-            return energy + fold(product * source[i])
+            result = near_product(i)
+            target[i] = result
+            return energy + fold(result * source[i])
         return lax.fori_loop(0, BLOCKS, one, zero, unroll=4)
 
     def join(near, i):
@@ -236,28 +243,23 @@
 
     lane = lax.broadcasted_iota(jnp.int32, (WIDTH, 2 * WIDTH), 1)
 
-    def both(block):
+    def tile(block):
         twice = jnp.concatenate([block, block], axis=1)
-        high = twice.astype(jnp.bfloat16).astype(jnp.float32)
-        return jnp.where(lane < WIDTH, high, twice - high).astype(jnp.bfloat16)
+        high, mid, low = [part.astype(jnp.float32) for part in split(twice)]
+        pieces = [jnp.where(lane < WIDTH, high, other) for other in (mid, low)]
+        return jnp.concatenate(pieces, axis=1).astype(jnp.bfloat16)
 
     def near_setup(i, carry):
-        blocks = [diagonal[i]] + [nearby[i, k] for k in range(LOCAL)]
-        for s, block in enumerate(blocks):
-            near_lhs[i, :, pl.ds(s * 2 * WIDTH, 2 * WIDTH)] = both(block)
-        for s in range(0, SOURCES, 2):
-            pair = jnp.concatenate([blocks[s], blocks[min(s + 1, SOURCES - 1)]], axis=1)
-            near_lhs[i, :, pl.ds((SOURCES * 2 + s) * WIDTH, 2 * WIDTH)] = pair.astype(jnp.bfloat16)
+        near_lhs[i, 0] = tile(diagonal[i])
+        for k in range(LOCAL):
+            near_lhs[i, k + 1] = tile(nearby[i, k])
         return carry
 
     lax.fori_loop(0, BLOCKS, near_setup, 0, unroll=2)
 
     def far_setup(t, carry):
         for e in range(CROSS):
-            block = remote[0, e, t]
-            far_lhs[e, t, :, pl.ds(0, 2 * WIDTH)] = both(block)
-            twice = jnp.concatenate([block, block], axis=1)
-            far_lhs[e, t, :, pl.ds(2 * WIDTH, 2 * WIDTH)] = twice.astype(jnp.bfloat16)
+            far_lhs[e, t] = tile(remote[0, e, t])
         return carry
 
     lax.fori_loop(0, SLOTS, far_setup, 0, unroll=2)
@@ -399,8 +401,9 @@
             + [
                 pltpu.VMEM(field, bf16),
                 pltpu.VMEM(field, bf16),
-                pltpu.VMEM((BLOCKS, WIDTH, 1024), bf16),
-                pltpu.VMEM((CROSS, SLOTS, WIDTH, 256), bf16),
+                pltpu.VMEM(field, bf16),
+                pltpu.VMEM((BLOCKS, SOURCES, WIDTH, DEPTH), bf16),
+                pltpu.VMEM((CROSS, SLOTS, WIDTH, DEPTH), bf16),
                 pltpu.VMEM((CROSS, SLOTS + 1, WIDTH, RHS), f32),
                 pltpu.VMEM((3, CROSS, SLOTS, WIDTH, RHS), f32),
                 pltpu.VMEM((3, CROSS, SLOTS, WIDTH, RHS), f32),
@@ -416,7 +419,7 @@
                 pltpu.SemaphoreType.DMA((2,)),
             ],
             compiler_params=pltpu.CompilerParams(
-                collective_id=0, has_side_effects=True, vmem_limit_bytes=51 * 1024 * 1024
+                collective_id=0, has_side_effects=True, vmem_limit_bytes=54_000_000
             ),
             name="relay",
         )(neighbors.T, pairs, right_side, diagonal_matrices, nearby_coupling_blocks, remote_coupling_blocks)

time: 59.7 us -> 58.7 us (0.983)
  local copies, waits for them, and re-layouts: 2.41 us -> 1.37 us
    unnamed x6, local copies, waits for them, and re-layouts: 2.4 us -> 1.36 us
where the time goes in v5:
time: 58.7 us; the launch traced here: 58.5 us
  Pallas kernels  55.2 us (94%)
  local copies, waits for them, and re-layouts  1.37 us (2%)
  other arithmetic  1.26 us (2%)
  between operations  0.67 us (1%)
    pallas_call x1, Pallas kernels, local(): pl.pallas_call(functools.partial(kernel, nx, nz), out_shape=(jax.ShapeDty...  55.2 us
    unnamed x6, local copies, waits for them, and re-layouts  1.36 us
    add x1, other arithmetic, local(): right_side - factors[3] * w0 - factors[4] * w1 + (factors[5] * z0 + facto...  1.26 us

profile of v5, /device:TPU:1, one launch (start us, length us, event | category | flops | bytes accessed | tf_op | source)
XLA Modules:
  0.0 58.5 jit_solution(1967461680145482187)
XLA Ops:
  0.6 0.0 copy-start
  0.6 0.7 %copy-done = s32[1,3,2,8]{3,2,1,0:T(2,128)S(1)} copy-done((s32[1,3,2,8]{3,2,1,0:T(2,128)S(1)}, s32[1,3,2,8]{3,2,1,0:T(2,128)}, u32[]{:S(2)}) %copy-start) | copy-done | bytes 216
  1.3 0.0 copy-start.1
  1.3 0.7 %copy-done.1 = s32[16,4]{0,1:T(4,128)S(1)} copy-done((s32[16,4]{0,1:T(4,128)S(1)}, s32[16,4]{0,1:T(4,128)}, u32[]{:S(2)}) %copy-start.1) | copy-done | bytes 280
  2.0 0.0 copy-start.2
  2.0 55.2 %relay.1 = (f32[16,64,128]{2,1,0:T(8,128)S(1)}, f32[16,64,128]{2,1,0:T(8,128)S(1)}, f32[16,64,128]{2,1,0:T(8,128)S(1)}, f32[16,64,128]{2,1,0:T(8,128)S(1)}, f32[8,128]{1,0:T(8,128)S(1)}) custom-call(s32[4,16]{1,0:T(4,128)S(1)} %bitcast.13, s32[1,3,2,8]{3,2,1,0:T(2,128)S(1)} %copy-done, f32[16,64,128]{2,1,0:T(8,128)} %right_side_in.1, ...), custom_call_target="tpu_custom_call" | custom-call | tf_op jit(solution)/shard_map/relay/pallas_call | solution.py:388
  57.3 0.0 copy-done.2
  57.3 1.3 %add_add_fusion = (f32[16,64,128]{2,1,0:T(8,128)}, f32[16,64,128]{2,1,0:T(8,128)}) fusion(f32[16,64,128]{2,1,0:T(8,128)S(1)} %get-tuple-element.11, f32[16,64,128]{2,1,0:T(8,128)S(1)} %get-tuple-element.10, f32[16,64,128]{2,1,0:T(8,128)S(1)} %get-tuple-element.9, f32[16,64,128]{2,1,0:T(8,128)S(1)} %copy-done.2, f32[16,64,128]{2,1,0:T(8,128)S(1)} %get-tuple-element.8, ...), kind=kLoop, calls=%fused_computation | loop fusion | flops 1703936 | bytes 3673088 | tf_op jit(solution)/shard_map/add | solution.py:427
  (1 shorter events, 0.0 us)
Async XLA Ops:
  0.6 0.7 %copy-start = (s32[1,3,2,8]{3,2,1,0:T(2,128)S(1)}, s32[1,3,2,8]{3,2,1,0:T(2,128)}, u32[]{:S(2)}) copy-start(s32[1,3,2,8]{3,2,1,0:T(2,128)} %pairs_in.1) | copy-start | bytes 580
  1.3 0.7 %copy-start.1 = (s32[16,4]{0,1:T(4,128)S(1)}, s32[16,4]{0,1:T(4,128)}, u32[]{:S(2)}) copy-start(s32[16,4]{0,1:T(4,128)} %param.9) | copy-start | bytes 772
  2.0 55.3 %copy-start.2 = (f32[16,64,128]{2,1,0:T(8,128)S(1)}, f32[16,64,128]{2,1,0:T(8,128)}, u32[]{:S(2)}) copy-start(f32[16,64,128]{2,1,0:T(8,128)} %right_side_in.1) | copy-start | bytes 1572868

commit v6 on v5

--- a/solution.py
+++ b/solution.py
@@ -50,9 +50,9 @@
 
 def kernel(
     nx, nz,
-    neighbors_in, pairs_in, right_side_in, diagonal_in, nearby_in, remote_in,
+    table_in, right_side_in, diagonal_in, nearby_in, remote_in,
     w0, w1, z0, z1, factors,
-    neighbors, pairs, right_side, diagonal, nearby, remote,
+    table, right_side, diagonal, nearby, remote,
     x_high, x_mid, x_low, near_lhs, far_lhs, coupled,
     sent, received, first_sums, second_sums, inverse,
     in_sem, send_sem, recv_sem, first_send, first_recv, second_send, second_recv,
@@ -83,9 +83,8 @@
         pltpu.make_async_copy(source, target, in_sem.at[n])
         for n, (source, target) in enumerate(
             (
-                (pairs_in, pairs),
+                (table_in, table),
                 (right_side_in, right_side),
-                (neighbors_in, neighbors),
                 (diagonal_in, diagonal),
                 (nearby_in, nearby),
                 (remote_in, remote),
@@ -115,7 +114,7 @@
     def gather(op, half, q, block):
         for e in LEVEL_ORDER:
             t = slot_of(half, q, e)
-            sent[op, e, t] = block(jnp.maximum(pairs[0, e, 0, t], 0))
+            sent[op, e, t] = block(jnp.maximum(table[e, 0, t], 0))
 
     def send(op, half, q):
         for e in LEVEL_ORDER:
@@ -179,7 +178,7 @@
             store[i] = part
 
     def near_product(i):
-        sources = [i] + [jnp.bitwise_and(neighbors[k, i], BLOCKS - 1) for k in range(LOCAL)]
+        sources = [i] + [jnp.bitwise_and(table[CROSS + k // 2, k % 2, i], BLOCKS - 1) for k in range(LOCAL)]
         parts = [(x_high[j], x_mid[j], x_low[j]) for j in sources]
         return product([near_lhs[i, s] for s in range(SOURCES)], parts)
 
@@ -204,7 +203,7 @@
         def one(q, carry):
             slots, products = far_step(op, 0, q)
             for e in range(CROSS):
-                own = pairs[0, e, 0, slots[e]]
+                own = table[e, 0, slots[e]]
                 twice = 2.0 * fold(products[e] * source[jnp.maximum(own, 0)])
                 carry = carry + jnp.where(own >= 0, twice, 0.0)
             return carry
@@ -266,7 +265,7 @@
 
     for e in range(CROSS):
         coupled[e, SLOTS] = jnp.zeros((WIDTH, RHS), jnp.float32)
-        owns = [pairs[0, e, 0, t] for t in range(SLOTS)]
+        owns = [table[e, 0, t] for t in range(SLOTS)]
 
         def invert(i, carry):
             found = jnp.int32(SLOTS)
@@ -385,14 +384,15 @@
         field = (BLOCKS, WIDTH, RHS)
         vmem = pl.BlockSpec(memory_space=pltpu.VMEM)
         f32, bf16 = jnp.float32, jnp.bfloat16
+        own_pairs = jnp.pad(pairs[0], ((0, 0), (0, 0), (0, BLOCKS - SLOTS)))
+        table = jnp.concatenate([own_pairs, neighbors.T.reshape(LOCAL // 2, 2, BLOCKS)])
         w0, w1, z0, z1, factors = pl.pallas_call(
             functools.partial(kernel, nx, nz),
             out_shape=(jax.ShapeDtypeStruct(field, f32),) * 4 + (jax.ShapeDtypeStruct((8, RHS), f32),),
-            in_specs=[pl.BlockSpec(memory_space=pl.ANY)] * 6,
+            in_specs=[pl.BlockSpec(memory_space=pl.ANY)] * 5,
             out_specs=(vmem,) * 5,
             scratch_shapes=[
-                pltpu.SMEM((LOCAL, BLOCKS), jnp.int32),
-                pltpu.SMEM(pairs.shape, jnp.int32),
+                pltpu.SMEM(table.shape, jnp.int32),
                 pltpu.VMEM(field, f32),
                 pltpu.VMEM(diagonal_matrices.shape, f32),
                 pltpu.VMEM(nearby_coupling_blocks.shape, f32),
@@ -410,7 +410,7 @@
                 pltpu.VMEM((2, n1, 8, RHS), f32),
                 pltpu.VMEM((2, n2, 8, RHS), f32),
                 pltpu.SMEM((CROSS * BLOCKS,), jnp.int32),
-                pltpu.SemaphoreType.DMA((6,)),
+                pltpu.SemaphoreType.DMA((5,)),
                 pltpu.SemaphoreType.DMA((3, CROSS, SLOTS)),
                 pltpu.SemaphoreType.DMA((3, CROSS, SLOTS)),
                 pltpu.SemaphoreType.DMA((2,)),
@@ -422,7 +422,7 @@
                 collective_id=0, has_side_effects=True, vmem_limit_bytes=54_000_000
             ),
             name="relay",
-        )(neighbors.T, pairs, right_side, diagonal_matrices, nearby_coupling_blocks, remote_coupling_blocks)
+        )(table, right_side, diagonal_matrices, nearby_coupling_blocks, remote_coupling_blocks)
         solution = (factors[0] * right_side - factors[1] * w0) - factors[2] * w1
         residual = ((right_side - factors[3] * w0) - factors[4] * w1) + (factors[5] * z0 + factors[2] * z1)
         return solution, residual

time: 58.7 us -> 58.1 us (0.990)
  local copies, waits for them, and re-layouts: 1.37 us -> 0.01 us
  other arithmetic: 1.26 us -> 2.03 us
    unnamed x6 -> x2, local copies, waits for them, and re-layouts: 1.36 us -> 0.01 us
    concatenate x0 -> x1, other arithmetic: none -> 0.76 us  [local(): jnp.concatenate([own_pairs, neighbors.T.reshape(LOCAL // 2, 2, BLOCKS)])]
where the time goes in v6:
time: 58.1 us; the launch traced here: 57.9 us
  Pallas kernels  55.2 us (95%)
  other arithmetic  2.03 us (3%)
  between operations  0.66 us (1%)
    pallas_call x1, Pallas kernels, local(): pl.pallas_call(functools.partial(kernel, nx, nz), out_shape=(jax.ShapeDty...  55.2 us
    add x1, other arithmetic, local(): right_side - factors[3] * w0 - factors[4] * w1 + (factors[5] * z0 + facto...  1.26 us

profile of v6, /device:TPU:1, one launch (start us, length us, event | category | flops | bytes accessed | tf_op | source)
XLA Modules:
  0.0 57.9 jit_solution(769490362862421406)
XLA Ops:
  0.6 0.0 copy-start
  0.6 0.8 %pad_add_fusion.table_in = s32[5,2,16]{2,1,0:T(2,128)S(1)} fusion(s32[3,2,8]{2,1,0:T(2,128)} %bitcast.16, s32[2,2,16]{2,1,0:T(2,128)} %bitcast.17), kind=kLoop, calls=%fused_computation.2 | loop fusion | flops 160 | bytes 1088 | tf_op jit(solution)/shard_map/concatenate | solution.py:388
  1.4 55.2 %relay.1 = (f32[16,64,128]{2,1,0:T(8,128)S(1)}, f32[16,64,128]{2,1,0:T(8,128)S(1)}, f32[16,64,128]{2,1,0:T(8,128)S(1)}, f32[16,64,128]{2,1,0:T(8,128)S(1)}, f32[8,128]{1,0:T(8,128)S(1)}) custom-call(s32[5,2,16]{2,1,0:T(2,128)S(1)} %pad_add_fusion.table_in, f32[16,64,128]{2,1,0:T(8,128)} %right_side_in.1, f32[16,64,64]{2,1,0:T(8,128)} %diagonal_in.1, ...), custom_call_target="tpu_custom_call" | custom-call | tf_op jit(solution)/shard_map/relay/pallas_call | solution.py:389
  56.7 0.0 copy-done
  56.7 1.3 %add_add_fusion = (f32[16,64,128]{2,1,0:T(8,128)}, f32[16,64,128]{2,1,0:T(8,128)}) fusion(f32[16,64,128]{2,1,0:T(8,128)S(1)} %get-tuple-element.11, f32[16,64,128]{2,1,0:T(8,128)S(1)} %get-tuple-element.10, f32[16,64,128]{2,1,0:T(8,128)S(1)} %get-tuple-element.9, f32[16,64,128]{2,1,0:T(8,128)S(1)} %copy-done, f32[16,64,128]{2,1,0:T(8,128)S(1)} %get-tuple-element.8, ...), kind=kLoop, calls=%fused_computation | loop fusion | flops 1703936 | bytes 3673088 | tf_op jit(solution)/shard_map/add | solution.py:427
  (1 shorter events, 0.0 us)
Async XLA Ops:
  0.6 56.0 %copy-start = (f32[16,64,128]{2,1,0:T(8,128)S(1)}, f32[16,64,128]{2,1,0:T(8,128)}, u32[]{:S(2)}) copy-start(f32[16,64,128]{2,1,0:T(8,128)} %right_side_in.1) | copy-start | bytes 1572868

commit v7 on v6

--- a/solution.py
+++ b/solution.py
@@ -199,21 +199,21 @@
             return carry
         lax.fori_loop(0, HALF, one, 0, unroll=4)
 
-    def energy_half(op, source, energy):
+    def energy_half(op, source, weigh, energy):
         def one(q, carry):
             slots, products = far_step(op, 0, q)
             for e in range(CROSS):
                 own = table[e, 0, slots[e]]
-                twice = 2.0 * fold(products[e] * source[jnp.maximum(own, 0)])
+                twice = 2.0 * fold(weigh(products[e], source[jnp.maximum(own, 0)]))
                 carry = carry + jnp.where(own >= 0, twice, 0.0)
             return carry
         return lax.fori_loop(0, HALF, one, energy, unroll=4)
 
-    def near_energy(target, source):
+    def near_energy(target, source, weigh):
         def one(i, energy):
             result = near_product(i)
             target[i] = result
-            return energy + fold(result * source[i])
+            return energy + fold(weigh(result, source[i]))
         return lax.fori_loop(0, BLOCKS, one, zero, unroll=4)
 
     def join(near, i):
@@ -288,7 +288,7 @@
             return carry
         lax.fori_loop(0, BLOCKS, one, 0, unroll=4)
 
-    energy = energy_half(0, right_side, near_energy(w0, right_side))
+    energy = energy_half(0, right_side, jnp.multiply, near_energy(w0, right_side, jnp.multiply))
     sum_start(0, 0, rows_of([gamma, energy]))
     far_half(0, 1)
 
@@ -312,6 +312,9 @@
 
     send_half(2, 0, lambda j: w0[j] - step0 * join(z0, j))
 
+    def scaled(image, value):
+        return (step0 * (step0 * image)) * (step0 * value)
+
     def z0_join(i, carry):
         zz, wa = join(z0, i), w0[i]
         wb = wa - step0 * zz
@@ -319,11 +322,12 @@
         z0[i] = zz
         w1[i] = wb
         put(i, wb)
+        wa, wb, zz = step0 * wa, step0 * wb, step0 * (step0 * zz)
         terms = (r * r, r * wb, wb * wb, wb * wa, wa * wa, wb * zz, wa * zz)
         return tuple(c + fold(t) for c, t in zip(carry, terms))
 
     sums = lax.fori_loop(0, BLOCKS, z0_join, (zero,) * 7, unroll=2)
-    energy = energy_half(2, w1, near_energy(z1, w1))
+    energy = energy_half(2, w1, scaled, near_energy(z1, w1, scaled))
     sum_start(1, 0, rows_of(list(sums) + [energy]))
     send_half(2, 1, lambda j: w1[j])
     sum_start(1, 1, sum_finish(1, 0))
@@ -336,21 +340,22 @@
     lax.fori_loop(0, BLOCKS, z1_join, 0, unroll=4)
     totals = sum_finish(1, 1)
     gamma1, delta1, w1w1, w1w0, w0w0, w1z0, w0z0, w1aw1 = [totals[k : k + 1] for k in range(8)]
-    rw0 = delta0 - step0 * w0w0
+    rw0 = gamma0 - w0w0
     ratio1 = gamma1 / gamma0
-    step1 = gamma1 / (delta1 - ratio1 * gamma1 / step0)
+    pace1 = gamma1 / (delta1 - ratio1 * gamma1)
     gamma2 = (
         gamma1
-        - 2.0 * step1 * (delta1 + ratio1 * rw0)
-        + step1 * step1 * (w1w1 + 2.0 * ratio1 * w1w0 + ratio1 * ratio1 * w0w0)
+        - 2.0 * pace1 * (delta1 + ratio1 * rw0)
+        + pace1 * pace1 * (w1w1 + 2.0 * ratio1 * w1w0 + ratio1 * ratio1 * w0w0)
     )
     delta2 = (
         delta1
-        - 2.0 * step1 * (w1w1 + ratio1 * w1w0)
-        + step1 * step1 * (w1aw1 + 2.0 * ratio1 * w1z0 + ratio1 * ratio1 * w0z0)
+        - 2.0 * pace1 * (w1w1 + ratio1 * w1w0)
+        + pace1 * pace1 * (w1aw1 + 2.0 * ratio1 * w1z0 + ratio1 * ratio1 * w0z0)
     )
     ratio2 = gamma2 / gamma1
-    step2 = gamma2 / (delta2 - ratio2 * gamma2 / step1)
+    pace2 = gamma2 / (delta2 - ratio2 * gamma2 / pace1)
+    step1, step2 = step0 * pace1, step0 * pace2
     both_steps = step1 * step2
     factors[...] = jnp.concatenate(
         [

time: 58.1 us -> 58.1 us (level)
  no operation moved by 1% of the time
where the time goes in v7:
time: 58.1 us; the launch traced here: 57.9 us
  Pallas kernels  55.2 us (95%)
  other arithmetic  2.03 us (3%)
  between operations  0.66 us (1%)
    pallas_call x1, Pallas kernels, local(): pl.pallas_call(functools.partial(kernel, nx, nz), out_shape=(jax.ShapeDty...  55.2 us
    add x1, other arithmetic, local(): right_side - factors[3] * w0 - factors[4] * w1 + (factors[5] * z0 + facto...  1.26 us

profile of v7, /device:TPU:1, one launch (start us, length us, event | category | flops | bytes accessed | tf_op | source)
XLA Modules:
  0.0 57.9 jit_solution(1487817574777216071)
XLA Ops:
  0.6 0.0 copy-start
  0.6 0.8 %pad_add_fusion.table_in = s32[5,2,16]{2,1,0:T(2,128)S(1)} fusion(s32[3,2,8]{2,1,0:T(2,128)} %bitcast.16, s32[2,2,16]{2,1,0:T(2,128)} %bitcast.17), kind=kLoop, calls=%fused_computation.2 | loop fusion | flops 160 | bytes 1088 | tf_op jit(solution)/shard_map/concatenate | solution.py:393
  1.4 55.2 %relay.1 = (f32[16,64,128]{2,1,0:T(8,128)S(1)}, f32[16,64,128]{2,1,0:T(8,128)S(1)}, f32[16,64,128]{2,1,0:T(8,128)S(1)}, f32[16,64,128]{2,1,0:T(8,128)S(1)}, f32[8,128]{1,0:T(8,128)S(1)}) custom-call(s32[5,2,16]{2,1,0:T(2,128)S(1)} %pad_add_fusion.table_in, f32[16,64,128]{2,1,0:T(8,128)} %right_side_in.1, f32[16,64,64]{2,1,0:T(8,128)} %diagonal_in.1, ...), custom_call_target="tpu_custom_call" | custom-call | tf_op jit(solution)/shard_map/relay/pallas_call | solution.py:394
  56.7 0.0 copy-done
  56.7 1.3 %add_add_fusion = (f32[16,64,128]{2,1,0:T(8,128)}, f32[16,64,128]{2,1,0:T(8,128)}) fusion(f32[16,64,128]{2,1,0:T(8,128)S(1)} %get-tuple-element.11, f32[16,64,128]{2,1,0:T(8,128)S(1)} %get-tuple-element.10, f32[16,64,128]{2,1,0:T(8,128)S(1)} %get-tuple-element.9, f32[16,64,128]{2,1,0:T(8,128)S(1)} %copy-done, f32[16,64,128]{2,1,0:T(8,128)S(1)} %get-tuple-element.8, ...), kind=kLoop, calls=%fused_computation | loop fusion | flops 1703936 | bytes 3673088 | tf_op jit(solution)/shard_map/add | solution.py:432
  (1 shorter events, 0.0 us)
Async XLA Ops:
  0.6 56.0 %copy-start = (f32[16,64,128]{2,1,0:T(8,128)S(1)}, f32[16,64,128]{2,1,0:T(8,128)}, u32[]{:S(2)}) copy-start(f32[16,64,128]{2,1,0:T(8,128)} %right_side_in.1) | copy-start | bytes 1572868
